TPU v7x, 32 devices: a whole 2x2x4 slice. The times are simulated.
32 devices in a mesh: groups: 2 (over x), seq: 16 (over z, y, core).
Axes of the slice: x: 2, y: 2, z: 4, core: 2. Of those that a mesh axis runs over, the one named last changes fastest.
Arguments:
- delta_query: bfloat16 [4096, 8, 128], P(('groups', 'seq')), parts along dimension 0, may hold values from -6 to 6
- delta_key: bfloat16 [4096, 8, 128], P(('groups', 'seq')), parts along dimension 0, may hold values from -6 to 6
- delta_value: bfloat16 [4096, 16, 128], P(('groups', 'seq')), parts along dimension 0, may hold values from -6 to 6
- log_decay: float32 [4096, 16], P(('groups', 'seq')), parts along dimension 0, may hold values from -0.8 to 0
- write_logit: float32 [4096, 16], P(('groups', 'seq')), parts along dimension 0, may hold values from -8 to 6
- output_gate: bfloat16 [4096, 16, 128], P(('groups', 'seq')), parts along dimension 0, may hold values from -6 to 6
- attn_query: bfloat16 [4096, 8, 256], P(('groups', 'seq')), parts along dimension 0, may hold values from -96 to 96
- attn_key: bfloat16 [4096, 2, 256], P(('groups', 'seq')), parts along dimension 0, may hold values from -5 to 5
- attn_value: bfloat16 [4096, 2, 256], P(('groups', 'seq')), parts along dimension 0, may hold values from -6 to 6
- attn_gate: bfloat16 [4096, 8, 256], P(('groups', 'seq')), parts along dimension 0, may hold values from -6 to 6
- doc_ids: int32 [64], P('groups'), parts along dimension 0, may hold values from 0 to 7, never falling along the last dimension, each value on 1 to 8 neighbouring positions
Outputs:
- delta_out: bfloat16 [4096, 16, 128], P(('groups', 'seq')), parts along dimension 0
- attn_out: bfloat16 [4096, 8, 256], P(('groups', 'seq')), parts along dimension 0
There are 2 independent parts, one for each index of `groups`. A program takes and returns all parts, laid end to end along the dimension named above; each array names one. Nothing has to cross between parts.
Inputs may be any that keep to these rules, and one draw needn't show every extreme that they name: `doc_ids`: never falls from block to block; each document covers 1 to 8 blocks, and one covers exactly 8.
All inputs are finite; a program needn't handle non-finite values.
Results may differ from a plain program's by a relative error of at most 0.0055.
Values may be sent and summed in bfloat16 or wider, within the bound.
A program may use at most 320 MiB of HBM per device.

v0:
```python
import jax
import jax.numpy as jnp
from jax import lax
from jax.sharding import PartitionSpec as P

BLK = 64
SPAN = 4


highest = lax.Precision.HIGHEST


def prefix_2(shard, axis, join, neutral):
    place = lax.axis_index(axis)
    gathered = jax.tree.map(
        lambda a, kind: lax.all_gather(a.astype(kind), axis), shard, (jnp.bfloat16, jnp.bfloat16)
    )
    state = jax.tree.map(lambda a, e: jnp.zeros_like(a) + jnp.asarray(e, a.dtype), shard, neutral)

    def one(hop, state):
        return join(
            state,
            jax.tree.map(
                lambda a, own: lax.dynamic_index_in_dim(a, hop, 0, False).astype(own.dtype),
                gathered,
                shard,
            ),
        )

    return lax.fori_loop(0, place, one, state)


def shifted(block, axis, distance):
    devices = range(lax.axis_size(axis))
    route = [(i - distance, i) for i in devices if i - distance in devices]
    return lax.ppermute(block, axis, route)


def unit_rows(vectors):
    vectors = vectors.astype(jnp.float32)
    return vectors * lax.rsqrt(jnp.sum(vectors * vectors, axis=-1, keepdims=True) + 1e-06)


def block_terms(queries, key_rows, values, decay_rows, writes):
    length = queries.shape[1]
    head_width = queries.shape[2]
    cumulative = jnp.cumsum(decay_rows, axis=1)
    rowpos = lax.broadcasted_iota(jnp.int32, (length, length), 0)
    colpos = lax.broadcasted_iota(jnp.int32, (length, length), 1)
    spread = cumulative[:, :, None] - cumulative[:, None, :]
    strict = jnp.exp(jnp.where(colpos < rowpos, spread, -jnp.inf))
    inclusive = jnp.exp(jnp.where(colpos <= rowpos, spread, -jnp.inf))
    key_key = jnp.einsum("htd,hsd->hts", key_rows, key_rows, precision=highest)
    query_key = jnp.einsum("htd,hsd->hts", queries, key_rows, precision=highest)
    system = jnp.eye(length, dtype=jnp.float32) + strict * writes[:, None, :] * key_key
    growth = jnp.exp(cumulative)
    stacked = jnp.concatenate([values, growth[:, :, None] * key_rows], axis=2)
    solved = lax.linalg.triangular_solve(
        system, stacked, left_side=True, lower=True, unit_diagonal=True
    )
    base_update = solved[:, :, :head_width]
    base_write = solved[:, :, head_width:]
    mixing = inclusive * writes[:, None, :] * query_key
    tail_weight = jnp.exp(cumulative[:, -1:] - cumulative) * writes
    return (growth, mixing, tail_weight, base_update, base_write)


def block_output(block_parts, queries, key_rows, state):
    growth, mixing, tail_weight, base_update, base_write = block_parts
    update = base_update - jnp.einsum("hsk,hvk->hsv", base_write, state, precision=highest)
    outputs = growth[:, :, None] * jnp.einsum("htk,hvk->htv", queries, state, precision=highest)
    outputs = outputs + jnp.einsum("hts,hsv->htv", mixing, update, precision=highest)
    end_state = growth[:, -1, None, None] * state + jnp.einsum(
        "hsv,hsk->hvk", tail_weight[:, :, None] * update, key_rows, precision=highest
    )
    return (outputs, end_state)


def gated_norm(outputs, gate_rows):
    factor = lax.rsqrt(jnp.mean(outputs * outputs, axis=-1, keepdims=True) + 1e-06)
    return (outputs * factor * jax.nn.silu(gate_rows.astype(jnp.float32))).astype(jnp.bfloat16)


def compose(earlier, latter):
    joined_map = jnp.einsum("hkj,hjl->hkl", earlier[0], latter[0], precision=highest)
    joined_offset = jnp.einsum("hvj,hjl->hvl", earlier[1], latter[0], precision=highest) + latter[1]
    return (joined_map, joined_offset)


def local(
    delta_query,
    delta_key,
    delta_value,
    log_decay,
    write_logit,
    output_gate,
    attn_query,
    attn_key,
    attn_value,
    attn_gate,
    doc_ids,
):
    position = lax.axis_index("seq")
    tok_rows = delta_query.shape[0]
    head_count = delta_value.shape[1]
    head_width = delta_value.shape[2]
    block_count = tok_rows // BLK
    group_ratio = head_count // delta_key.shape[1]
    window = lax.dynamic_slice_in_dim(
        jnp.concatenate([doc_ids[:1] - 1, doc_ids]), position * block_count, block_count + 1
    )
    local_docs = window[1:]
    carry_mask = (local_docs == window[:-1]).astype(jnp.float32)

    def heads_first(tensor):
        return tensor.reshape(block_count, BLK, head_count, head_width).transpose(0, 2, 1, 3)

    queries = heads_first(jnp.repeat(unit_rows(delta_query), group_ratio, axis=1))
    key_rows = heads_first(jnp.repeat(unit_rows(delta_key), group_ratio, axis=1))
    values = heads_first(delta_value.astype(jnp.float32))
    decay_rows = log_decay.reshape(block_count, BLK, head_count).transpose(0, 2, 1)
    writes = jax.nn.sigmoid(write_logit).reshape(block_count, BLK, head_count).transpose(0, 2, 1)
    block_parts = jax.vmap(block_terms)(queries, key_rows, values, decay_rows, writes)
    growth, mixing, tail_weight, base_update, base_write = block_parts
    identity = jnp.eye(head_width, dtype=jnp.float32)
    mapping = growth[:, :, -1, None, None] * identity - jnp.einsum(
        "bhsk,bhsj->bhkj", tail_weight[..., None] * base_write, key_rows, precision=highest
    )
    mapping = mapping * carry_mask[:, None, None, None]
    offset = jnp.einsum(
        "bhsv,bhsk->bhvk", tail_weight[..., None] * base_update, key_rows, precision=highest
    )
    zero_state = jnp.zeros((head_count, head_width, head_width), jnp.float32)
    identity_pair = (jnp.broadcast_to(identity, (head_count, head_width, head_width)), zero_state)

    def fold_block(running, block_map):
        return (compose(running, block_map), None)

    (device_map, device_offset), unused = lax.scan(fold_block, identity_pair, (mapping, offset))
    prefix = prefix_2((device_map, device_offset), "seq", compose, identity_pair)
    incoming = prefix[1]

    def advance(state, inputs):
        parts_here, block_q, block_k, block_keep = inputs
        outputs, end_state = block_output(parts_here, block_q, block_k, state * block_keep)
        return (end_state, outputs)

    unused_state, outputs = lax.scan(
        advance, incoming, (block_parts, queries, key_rows, carry_mask)
    )
    outputs = outputs.transpose(0, 2, 1, 3).reshape(tok_rows, head_count, head_width)
    delta_out = gated_norm(outputs, output_gate)
    kv_heads = attn_key.shape[1]
    attn_width = attn_key.shape[2]
    query_heads = attn_query.shape[1]
    group_size = query_heads // kv_heads
    score_scale = attn_width ** (-0.5)
    grouped = attn_query.reshape(tok_rows, kv_heads, group_size, attn_width)
    query_pos = position * tok_rows + jnp.arange(tok_rows, dtype=jnp.int32)
    query_doc = jnp.repeat(local_docs, BLK)

    def block_mask(source):
        key_pos = source * tok_rows + jnp.arange(tok_rows, dtype=jnp.int32)
        key_doc = jnp.repeat(
            lax.dynamic_slice_in_dim(doc_ids, jnp.maximum(source, 0) * block_count, block_count),
            BLK,
        )
        return (
            (source >= 0)
            & (key_doc[None, :] == query_doc[:, None])
            & (key_pos[None, :] <= query_pos[:, None])
        )

    def absorb(running, pair_rows, allowed):
        best, total, accum = running
        scores = (
            jnp.einsum("tgjd,sgd->gjts", grouped, pair_rows[0], preferred_element_type=jnp.float32)
            * score_scale
        )
        scores = jnp.where(allowed, scores, -jnp.inf)
        newbest = jnp.maximum(best, jnp.max(scores, axis=-1))
        weights = jnp.where(allowed, jnp.exp(scores - newbest[..., None]), 0.0)
        fading = jnp.exp(best - newbest)
        total = total * fading + jnp.sum(weights, axis=-1)
        accum = accum * fading.transpose(2, 0, 1)[..., None] + jnp.einsum(
            "gjts,sgd->tgjd",
            weights.astype(jnp.bfloat16),
            pair_rows[1],
            preferred_element_type=jnp.float32,
        )
        return (newbest, total, accum)

    def visit(running, pair_rows, source):
        allowed = block_mask(source)
        return absorb(running, pair_rows, allowed)

    start_best = jnp.full((kv_heads, group_size, tok_rows), -jnp.inf, jnp.float32)
    start_total = jnp.zeros((kv_heads, group_size, tok_rows), jnp.float32)
    start_accum = jnp.zeros((tok_rows, kv_heads, group_size, attn_width), jnp.float32)
    kv_pair = jnp.stack([attn_key, attn_value])
    running = visit((start_best, start_total, start_accum), kv_pair, position)

    def travel(step_index, carried):
        current, pair_rows = carried
        pair_rows = shifted(pair_rows, "seq", 1)
        return (visit(current, pair_rows, position - step_index - 1), pair_rows)

    (best, total, accum), unused_pair = lax.fori_loop(0, SPAN, travel, (running, kv_pair))
    gate_rows = jax.nn.sigmoid(attn_gate.astype(jnp.float32)).reshape(
        tok_rows, kv_heads, group_size, attn_width
    )
    attended = accum / total.transpose(2, 0, 1)[..., None] * gate_rows
    attn_out = attended.astype(jnp.bfloat16).reshape(tok_rows, query_heads, attn_width)
    return (delta_out, attn_out)


def solution(mesh):
    return jax.shard_map(
        local,
        mesh=mesh,
        in_specs=(
            P(("groups", "seq"), None, None),
            P(("groups", "seq"), None, None),
            P(("groups", "seq"), None, None),
            P(("groups", "seq"), None),
            P(("groups", "seq"), None),
            P(("groups", "seq"), None, None),
            P(("groups", "seq"), None, None),
            P(("groups", "seq"), None, None),
            P(("groups", "seq"), None, None),
            P(("groups", "seq"), None, None),
            P("groups"),
        ),
        out_specs=(P(("groups", "seq"), None, None), P(("groups", "seq"), None, None)),
        check_vma=False,
    )
```

profile of v0, /device:TPU:29, one launch (start us, length us, event | category | flops | bytes accessed | tf_op | source)
XLA Modules:
  0.0 445.4 jit_solution(8508076374560354706)
XLA Ops:
  12.7 1.8 fusion.59
  14.5 158.0 %custom-call.3 = f32[2,16,1,64,64]{3,4,2,1,0:T(8,128)} custom-call(f32[2,16,1,64,64]{4,3,2,1,0:T(8,128)S(1)} %fusion.59), custom_call_target="InvertDiagBlocksLowerTriangular" | custom-call | tf_op jit(solution)/shard_map/vmap()/triangular_solve | solution.py:58
  174.1 3.2 fusion.52
  177.3 5.1 %fusion.72 = f32[2,16,128,128]{2,3,1,0:T(8,128)} fusion(f32[2,16,64]{2,1,0:T(8,128)S(1)} %get-tuple-element.832, f32[2,16,64,256]{3,2,1,0:T(8,128)S(1)} %fusion.52, f32[2,64,16,128]{3,1,0,2:T(8,128)S(1)} %bitcast.219), kind=kOutput, calls=%fused_computation.104 | convolution fusion | flops 402915328 | bytes 4210688 | tf_op jit(solution)/shard_map/bhsv,bhsk->bhvk/dot_general | solution.py:130
  182.4 4.0 subtract_multiply_fusion
  186.5 13.8 %while.62 = (s32[]{:T(128)}, f32[16,128,128]{1,2,0:T(8,128)S(1)}, f32[16,128,128]{1,2,0:T(8,128)}, f32[2,16,128,128]{3,2,1,0:T(8,128)S(1)}, f32[2,16,128,128]{2,3,1,0:T(8,128)}, /*index=5*/s32[]{:T(128)}, s32[]{:T(128)}) while((s32[]{:T(128)}, f32[16,128,128]{1,2,0:T(8,128)S(1)}, f32[16,128,128]{1,2,0:T(8,128)}, ...), condition=%wide.region_3.4_spmd.clone, body=%wide.region_2.0_spmd.clone.sunk | while | flops 805830656 | bytes 19924088 | solution.py:139
  188.7 2.9 fusion.156
  191.7 1.9 convolution_bitcast_fusion.6
  195.5 2.9 fusion.156
  198.5 1.9 convolution_bitcast_fusion.6
  209.9 39.5 %while.61 = (s32[]{:T(128)}, f32[2,4,128]{2,1,0:T(4,128)S(1)}, f32[2,4,128]{2,1,0:T(4,128)S(1)}, f32[128,2,4,256]{3,0,2,1:T(8,128)S(1)}, bf16[2,128,2,256]{3,1,2...) while((s32[]{:T(128)}, f32[2,4,128]{2,1,0:T(4,128)S(1)}, ...), condition=%wide.region_15.16_spmd.clone, body=%wide.region_12.15_spmd.clone.sunk | while | flops 135990528 | bytes 6166865 | solution.py:208
  216.5 9.1 %collective-permute-done = bf16[2,128,2,256]{3,1,2,0:T(8,128)(2,1)S(1)} collective-permute-done((bf16[2,128,2,256]{3,1,2,0:T(8,128)(2,1)S(1)}, bf16[2,128,2,256]{3,1,2,0:T(8,128)(2,1)S(1)}, u32[]{:S(2)}, u32[]{:S(2)}) %collective-permute-start) | collective-permute-done | bytes 262176 | tf_op jit(solution)/shard_map/while/body/eval_jaxpr/ppermute | solution.py:36
  228.5 5.9 %collective-permute-done = bf16[2,128,2,256]{3,1,2,0:T(8,128)(2,1)S(1)} collective-permute-done((bf16[2,128,2,256]{3,1,2,0:T(8,128)(2,1)S(1)}, bf16[2,128,2,256]{3,1,2,0:T(8,128)(2,1)S(1)}, u32[]{:S(2)}, u32[]{:S(2)}) %collective-permute-start) | collective-permute-done | bytes 262176 | tf_op jit(solution)/shard_map/while/body/eval_jaxpr/ppermute | solution.py:36
  237.3 11.1 %collective-permute-done = bf16[2,128,2,256]{3,1,2,0:T(8,128)(2,1)S(1)} collective-permute-done((bf16[2,128,2,256]{3,1,2,0:T(8,128)(2,1)S(1)}, bf16[2,128,2,256]{3,1,2,0:T(8,128)(2,1)S(1)}, u32[]{:S(2)}, u32[]{:S(2)}) %collective-permute-start) | collective-permute-done | bytes 262176 | tf_op jit(solution)/shard_map/while/body/eval_jaxpr/ppermute | solution.py:36
  253.8 2.8 convolution_multiply_fusion.2
  256.6 26.8 %all-gather.5.cloned.1.call-done = bf16[256,128,128]{2,1,0:T(8,128)(2,1)} async-done(((bf16[16,128,128]{2,1,0:T(8,128)(2,1)}), bf16[256,128,128]{2,1,0:T(8,128)(2,1)}) %all-gather.5.cloned.1.call-update) | async-done | bytes 8388624 | tf_op jit(solution)/shard_map/all_gather | solution.py:16
  283.3 75.4 %all-gather.7.cloned.1.call-done = bf16[256,128,128]{2,1,0:T(8,128)(2,1)} async-done(((bf16[16,128,128]{2,1,0:T(8,128)(2,1)}), bf16[256,128,128]{2,1,0:T(8,128)(2,1)}) %all-gather.7.cloned.1.call-update) | async-done | bytes 8388624 | tf_op jit(solution)/shard_map/all_gather | solution.py:16
  358.8 49.7 %while.59 = (s32[]{:T(128)}, f32[16,128,128]{1,2,0:T(8,128)S(1)}, s32[]{:T(128)}, bf16[16,16,128,128]{3,2,1,0:T(8,128)(2,1)}, bf16[16,16,128,128]{3,2,1,0:T(8,128)(2,1)}, /*index=5*/s32[]{:T(128)}, s32[]{:T(128)}, s32[]{:T(128)}) while((s32[]{:T(128)}, f32[16,128,128]{1,2,0:T(8,128)S(1)}, s32[]{:T(128)}, bf16[16,16,128,128]{3,2,1,0:T(8,128)(2,1)}, ...), condition=%wide.region_5.6_spmd, body=%wide.region_4.5_spmd.sunk | while | flops 403177472 | bytes 7340159 | solution.py:30
  360.3 1.8 fusion.134
  363.6 1.8 fusion.134
  366.9 1.8 fusion.134
  376.9 1.8 fusion.134
  386.8 1.8 fusion.134
  406.7 1.8 fusion.134
  409.7 24.1 %while.60 = (s32[]{:T(128)}, f32[16,128,128]{2,1,0:T(8,128)S(1)}, f32[2,16,64,128]{3,2,1,0:T(8,128)}, f32[2,16,64]{2,1,0:T(8,128)S(1)}, f32[2]{0:T(128)S(1)}, /*...) while((s32[]{:T(128)}, f32[16,128,128]{2,1,0:T(8,128)S(1)}, ...), condition=%wide.region_8.9_spmd, body=%wide.region_7.8_spmd.sunk | while | flops 706478080 | bytes 24694664 | solution.py:148
  410.3 4.1 convolution_subtract_fusion.2
  415.2 2.8 fusion.145
  419.0 2.7 convolution_add_fusion.2
  422.4 4.1 convolution_subtract_fusion.2
  427.2 2.8 fusion.145
  431.1 2.7 convolution_add_fusion.2
  435.5 1.8 copy.117
  (250 shorter events, 84.7 us)
Async XLA Ops:
  7.2 276.2 %all-gather.5.cloned.1.call-start = ((), (), s32[]{:S(2)}) async-start(), calls=%async_computation | async-start | bytes 8912896 | tf_op jit(solution)/shard_map/all_gather | solution.py:16
  12.3 170.1 %copy-start = (f32[128,8,2,128]{3,0,2,1:T(8,128)}, f32[128,8,2,128]{3,0,2,1:T(8,128)S(1)}, u32[]{:S(2)}) copy-start(f32[128,8,2,128]{3,0,2,1:T(8,128)S(1)} %broadcast_in_dim.133) | copy-start | bytes 3145732
  12.7 161.0 %copy-start.19 = (s32[32]{0:T(128)S(1)}, s32[32]{0:T(128)}, u32[]{:S(2)}) copy-start(s32[32]{0:T(128)} %param.29) | copy-start | bytes 388
  177.3 5.1 %copy-start.4 = (f32[2,16,64,256]{3,2,1,0:T(8,128)}, f32[2,16,64,256]{3,2,1,0:T(8,128)S(1)}, u32[]{:S(2)}) copy-start(f32[2,16,64,256]{3,2,1,0:T(8,128)S(1)} %fusion.52) | copy-start | bytes 6291460
  186.8 1.9 copy-start.3
  193.6 1.9 copy-start.3
  200.4 1.4 copy-start.2
  200.4 2.4 copy-start.1
  201.4 157.3 %all-gather.7.cloned.1.call-start = ((), (), s32[]{:S(2)}) async-start(), calls=%async_computation.1 | async-start | bytes 8912896 | tf_op jit(solution)/shard_map/all_gather | solution.py:16
  201.8 2.2 copy-start.13
  204.5 2.6 copy-start.15
  204.5 2.7 copy-start.14
  204.6 1.0 copy-start.9
  207.3 1.6 copy-start.16
  207.3 1.6 copy-start.18
  209.9 3.6 collective-permute-start
  214.7 10.9 %collective-permute-start = (bf16[2,128,2,256]{3,1,2,0:T(8,128)(2,1)S(1)}, bf16[2,128,2,256]{3,1,2,0:T(8,128)(2,1)S(1)}, u32[]{:S(2)}, u32[]{:S(2)}) collective-permute-start(bf16[2,128,2,256]{3,1,2,0:T(8,128)(2,1)S(1)} %get-tuple-element.883), channel_id=1, source_target_pairs={{0,1},{1,2},{2,3},{3,4},{4,5},{5,6},{6,7},{7,8},{8,9},{9,10},{10,1... | collective-permute-start | bytes 786440 | tf_op jit(solution)/shard_map/while/body/eval_jaxpr/ppermute | solution.py:36
  226.6 7.7 %collective-permute-start = (bf16[2,128,2,256]{3,1,2,0:T(8,128)(2,1)S(1)}, bf16[2,128,2,256]{3,1,2,0:T(8,128)(2,1)S(1)}, u32[]{:S(2)}, u32[]{:S(2)}) collective-permute-start(bf16[2,128,2,256]{3,1,2,0:T(8,128)(2,1)S(1)} %get-tuple-element.883), channel_id=1, source_target_pairs={{0,1},{1,2},{2,3},{3,4},{4,5},{5,6},{6,7},{7,8},{8,9},{9,10},{10,1... | collective-permute-start | bytes 786440 | tf_op jit(solution)/shard_map/while/body/eval_jaxpr/ppermute | solution.py:36
  235.4 12.9 %collective-permute-start = (bf16[2,128,2,256]{3,1,2,0:T(8,128)(2,1)S(1)}, bf16[2,128,2,256]{3,1,2,0:T(8,128)(2,1)S(1)}, u32[]{:S(2)}, u32[]{:S(2)}) collective-permute-start(bf16[2,128,2,256]{3,1,2,0:T(8,128)(2,1)S(1)} %get-tuple-element.883), channel_id=1, source_target_pairs={{0,1},{1,2},{2,3},{3,4},{4,5},{5,6},{6,7},{7,8},{8,9},{9,10},{10,1... | collective-permute-start | bytes 786440 | tf_op jit(solution)/shard_map/while/body/eval_jaxpr/ppermute | solution.py:36
  249.4 2.7 copy-start.5
  252.1 1.6 copy-start.10
  408.5 1.2 copy-start.6
  409.7 4.7 %copy-start.7 = (f32[2,16,64,64]{3,2,1,0:T(8,128)S(1)}, f32[2,16,64,64]{3,2,1,0:T(8,128)}, u32[]{:S(2)}) copy-start(f32[2,16,64,64]{3,2,1,0:T(8,128)} %get-tuple-element.861) | copy-start | bytes 1572868 | tf_op jit(solution)/shard_map/while
  410.3 4.8 %copy-start.8 = (f32[2,16,64,128]{3,2,1,0:T(8,128)S(1)}, f32[2,16,64,128]{3,2,1,0:T(8,128)}, u32[]{:S(2)}) copy-start(f32[2,16,64,128]{3,2,1,0:T(8,128)} %get-tuple-element.860) | copy-start | bytes 3145732 | tf_op jit(solution)/shard_map/while
  410.3 4.8 %copy-start.11 = (f32[2,16,64,128]{3,2,1,0:T(8,128)S(1)}, f32[2,16,64,128]{3,2,1,0:T(8,128)}, u32[]{:S(2)}) copy-start(f32[2,16,64,128]{3,2,1,0:T(8,128)} %get-tuple-element.841) | copy-start | bytes 3145732 | tf_op jit(solution)/shard_map/while
  418.0 1.0 copy-start.12
  421.8 4.7 %copy-start.7 = (f32[2,16,64,64]{3,2,1,0:T(8,128)S(1)}, f32[2,16,64,64]{3,2,1,0:T(8,128)}, u32[]{:S(2)}) copy-start(f32[2,16,64,64]{3,2,1,0:T(8,128)} %get-tuple-element.861) | copy-start | bytes 1572868 | tf_op jit(solution)/shard_map/while
  422.4 4.8 %copy-start.8 = (f32[2,16,64,128]{3,2,1,0:T(8,128)S(1)}, f32[2,16,64,128]{3,2,1,0:T(8,128)}, u32[]{:S(2)}) copy-start(f32[2,16,64,128]{3,2,1,0:T(8,128)} %get-tuple-element.860) | copy-start | bytes 3145732 | tf_op jit(solution)/shard_map/while
  422.4 4.8 %copy-start.11 = (f32[2,16,64,128]{3,2,1,0:T(8,128)S(1)}, f32[2,16,64,128]{3,2,1,0:T(8,128)}, u32[]{:S(2)}) copy-start(f32[2,16,64,128]{3,2,1,0:T(8,128)} %get-tuple-element.841) | copy-start | bytes 3145732 | tf_op jit(solution)/shard_map/while
  430.0 1.0 copy-start.12
  433.8 3.6 copy-start.17
Sparse Core Ops, SparseCore 0:
  201.5 81.7 all-gather.4
  285.5 73.1 all-gather.6
where the time goes:
time: 447 us; the launch traced here: 445 us
  other arithmetic  168 us (38%)
  waiting for transfers between devices  130 us (29%)
  matrix products  78.4 us (18%)
  local copies, waits for them, and re-layouts  47.2 us (11%)
  between operations  14.5 us (3%)
  starting transfers between devices  5.25 us (1%)
    another operation x2, other arithmetic, block_terms(): lax.linalg.triangular_solve(system, stacked, left_side=True, lower=True,...  158 us
    all_gather x2, waiting for transfers between devices, prefix_2(): lax.all_gather(a.astype(kind), axis)  102 us
    dot_general x17, matrix products, compose(): jnp.einsum('hvj,hjl->hvl', earlier[1], latter[0], precision=highest)  33 us
    ppermute x4, waiting for transfers between devices, shifted(): return lax.ppermute(block, axis, route)  27.8 us
    dynamic_slice x30, local copies, waits for them, and re-layouts, one(): lax.dynamic_index_in_dim(a, hop, 0, False).astype(own.dtype)  20.4 us
  transfers between devices with their start and end apart: 6, of which 6 were waited for; matrix products, arithmetic and copies ran while one was open for 5% of the time, Pallas kernels for 0%

commit v1 on v0

v1 whole, which is shorter than its diff:
```python
import functools

import jax
import jax.numpy as jnp
from jax import lax
from jax.experimental import pallas as pl
from jax.experimental.pallas import tpu as pltpu
from jax.sharding import PartitionSpec as P

BLK = 64
SPAN = 4
F32 = jnp.float32
BF16 = jnp.bfloat16


def mm(a, b):
    return jnp.dot(a, b, preferred_element_type=F32)


def mm_nt(a, b):
    return lax.dot_general(a, b, (((1,), (1,)), ((), ())), preferred_element_type=F32)


def split(x):
    high = x.astype(BF16)
    return high, (x - high.astype(F32)).astype(BF16)


def mm3(a, b):
    ah, al = a
    bh, bl = b
    return mm(ah, bh) + (mm(ah, bl) + mm(al, bh))


def shifted(block, distance):
    devices = range(lax.axis_size("seq"))
    route = [(i - distance, i) for i in devices if i - distance in devices]
    return lax.ppermute(block, "seq", route)


def chunk_kernel(heads, ratio, q_ref, k_ref, v_ref, col_ref, row_ref, incl_ref, maps_ref, base_ref, read_ref):
    length = k_ref.shape[1]
    incl = incl_ref[...] > 0
    rows = lax.broadcasted_iota(jnp.int32, (length, length), 0)
    cols = lax.broadcasted_iota(jnp.int32, (length, length), 1)
    eye = (rows == cols).astype(F32)
    grams = []
    for j in range(heads // ratio):
        k = k_ref[j]
        grams.append((mm_nt(k, k), mm_nt(q_ref[j], k), k.T))
    decays, lows = [], []
    for h in range(heads):
        col = col_ref[0]
        row = row_ref[0]
        c_col, rk_col = col[:, 5 * h : 5 * h + 1], col[:, 5 * h + 1 : 5 * h + 2]
        c_row, bk_row = row[3 * h : 3 * h + 1], row[3 * h + 1 : 3 * h + 2]
        decay = jnp.exp(jnp.where(incl, c_col - c_row, -1e30)) * bk_row
        decays.append(decay)
        lows.append(jnp.where(rows > cols, decay * rk_col * grams[h // ratio][0], 0.0))
    inverses = [eye - jnp.where(rows // 2 == cols // 2, low, 0.0) for low in lows]
    size = 2
    while size < length:
        band = (rows // (2 * size) == cols // (2 * size)) & (rows // size != cols // size)
        parts = [split(x) for x in inverses]
        tops = [mm3(split(jnp.where(band, low, 0.0)), x) for low, x in zip(lows, parts)]
        inverses = [x - mm3(xp, split(t)) for x, xp, t in zip(inverses, parts, tops)]
        size *= 2
    for h in range(heads):
        k_gram, q_gram, k_t = grams[h // ratio]
        k, q, v = k_ref[h // ratio], q_ref[h // ratio], v_ref[h]
        col = col_ref[0]
        rq_col, gq_col, tk_col = (col[:, 5 * h + i : 5 * h + i + 1] for i in (2, 3, 4))
        gain = col_ref[0][length - 1 : length, 5 * heads + h : 5 * heads + h + 1]
        gk_row = row_ref[0][3 * h + 2 : 3 * h + 3]
        th, tl = split(inverses[h])
        update = mm(th, v) + mm(tl, v)
        wh, wl = split(inverses[h] * gk_row)
        write = mm(wh, k) + mm(wl, k)
        both = jnp.concatenate([write, update], axis=1)
        th, tl = split(both * tk_col)
        tail = mm(k_t, th) + mm(k_t, tl)
        maps_ref[h] = jnp.concatenate([eye * gain - tail[:, :length], tail[:, length:]], axis=1).astype(BF16)
        mix = (decays[h] * rq_col * q_gram).astype(BF16)
        mixed = mm(mix, both.astype(BF16))
        base_ref[h] = mixed[:, length:]
        read_ref[h] = (gq_col * q.astype(F32) - mixed[:, :length]).astype(BF16)


def compose_kernel(near_ref, far_ref, map_ref, off_ref, send_ref):
    width = near_ref.shape[1]
    for h in range(near_ref.shape[0]):
        joined = mm(near_ref[h, :, :width], far_ref[h])
        map_ref[h] = joined[:, :width].astype(BF16)
        off = joined[:, width:] + near_ref[h, :, width:].astype(F32)
        off_ref[h] = off
        send_ref[h] = off.astype(BF16)


def output_kernel(base_ref, read_ref, map_ref, off_ref, far_ref, gate_ref, out_ref):
    for h in range(base_ref.shape[0]):
        state = mm(map_ref[h], far_ref[h]) + off_ref[h]
        core = base_ref[h] + mm(read_ref[h], state.astype(BF16))
        factor = lax.rsqrt(jnp.mean(core * core, axis=-1, keepdims=True) + 1e-06)
        gate = gate_ref[h].astype(F32)
        out_ref[h] = (core * factor * (gate / (1.0 + jnp.exp(-gate)))).astype(BF16)


def attention_kernel(scale, runs, q_ref, mask_ref, gate_ref, *refs):
    out_ref = refs[-1]
    keys = jnp.concatenate([r[0, 0] for r in refs[:runs]], axis=0)
    values = jnp.concatenate([r[1, 0] for r in refs[:runs]], axis=0)
    for j in range(q_ref.shape[0]):
        scores = mm_nt(q_ref[j], keys) * scale + mask_ref[...]
        weights = jnp.exp(scores - jnp.max(scores, axis=-1, keepdims=True))
        total = jnp.sum(weights, axis=-1, keepdims=True)
        mixed = mm(weights.astype(BF16), values)
        gate = gate_ref[j].astype(F32)
        out_ref[j] = (mixed / total / (1.0 + jnp.exp(-gate))).astype(BF16)


def local(
    delta_query,
    delta_key,
    delta_value,
    log_decay,
    write_logit,
    output_gate,
    attn_query,
    attn_key,
    attn_value,
    attn_gate,
    doc_ids,
):
    position = lax.axis_index("seq")
    toks, key_heads, width = delta_key.shape
    heads = delta_value.shape[1]
    ratio = heads // key_heads
    blocks = toks // BLK
    kv_heads, attn_width = attn_key.shape[1:]
    query_heads = attn_query.shape[1]
    group = query_heads // kv_heads
    runs = SPAN + 1

    def heads_first(x):
        return x.transpose(1, 0, 2)

    kv = jnp.stack([heads_first(attn_key), heads_first(attn_value)])
    kv_runs = [shifted(kv, d) for d in range(SPAN, 0, -1)] + [kv]

    padded = jnp.concatenate([jnp.full((SPAN * blocks,), -1, doc_ids.dtype), doc_ids])
    window = lax.dynamic_slice_in_dim(padded, position * blocks, runs * blocks)
    key_doc = jnp.repeat(window, BLK)
    tok_doc = key_doc[SPAN * toks :]
    t = jnp.arange(toks, dtype=jnp.int32)
    key_pos = jnp.arange(runs * toks, dtype=jnp.int32) - SPAN * toks
    allowed = (key_doc[None, :] == tok_doc[:, None]) & (key_pos[None, :] <= t[:, None])
    mask = jnp.where(allowed, 0.0, -1e30).astype(F32)
    incl = allowed[:, SPAN * toks :].astype(F32)
    carried = (tok_doc == window[SPAN * blocks - 1]).astype(F32)[:, None]
    lasting = (tok_doc == tok_doc[-1]).astype(F32)[:, None]

    def unit_factor(x):
        x = x.astype(F32)
        return jnp.repeat(lax.rsqrt(jnp.sum(x * x, axis=-1) + 1e-06), ratio, axis=1)

    cum = jnp.cumsum(log_decay, axis=0)
    writes = jax.nn.sigmoid(write_logit)
    rq, rk = unit_factor(delta_query), unit_factor(delta_key)
    grown = jnp.exp(cum) * carried
    tail = jnp.exp(cum[-1:] - cum) * writes * lasting
    per = 4
    steps = heads // per
    cols = jnp.stack([cum, rk, rq, grown * rq, tail * rk], axis=-1)
    cols = cols.reshape(toks, steps, per * 5)
    cols = jnp.concatenate([cols, grown.reshape(toks, steps, per)], axis=-1).transpose(1, 0, 2)
    rowv = jnp.stack([cum, writes * rk, grown * rk], axis=-1)
    rowv = rowv.reshape(toks, steps, per * 3).transpose(1, 2, 0)

    def lead(n, *rest):
        return pl.BlockSpec((n, *rest), lambda i: (i,) + (0,) * len(rest))

    whole = pl.BlockSpec((toks, toks), lambda i: (0, 0))
    params = pltpu.CompilerParams(vmem_limit_bytes=32 * 1024 * 1024)
    maps, base, read = pl.pallas_call(
        functools.partial(chunk_kernel, per, ratio),
        grid=(steps,),
        in_specs=[
            lead(per // ratio, toks, width),
            lead(per // ratio, toks, width),
            lead(per, toks, width),
            lead(1, toks, per * 6),
            lead(1, per * 3, toks),
            whole,
        ],
        out_specs=[lead(per, width, 2 * width), lead(per, toks, width), lead(per, toks, width)],
        out_shape=[
            jax.ShapeDtypeStruct((heads, width, 2 * width), BF16),
            jax.ShapeDtypeStruct((heads, toks, width), F32),
            jax.ShapeDtypeStruct((heads, toks, width), BF16),
        ],
        compiler_params=params,
        cost_estimate=pl.CostEstimate(flops=4 * 10**9, bytes_accessed=4 * 10**6, transcendentals=10**6),
        name="delta_chunk",
    )(heads_first(delta_query), heads_first(delta_key), heads_first(delta_value), cols, rowv, incl)

    near, far = shifted(maps, 1), shifted(maps, 2)

    kv_spec = pl.BlockSpec((2, 1, toks, attn_width), lambda i: (0, i, 0, 0))
    attended = pl.pallas_call(
        functools.partial(attention_kernel, attn_width ** (-0.5), runs),
        grid=(kv_heads,),
        in_specs=[
            lead(group, toks, attn_width),
            pl.BlockSpec(mask.shape, lambda i: (0, 0)),
            lead(group, toks, attn_width),
        ]
        + [kv_spec] * runs,
        out_specs=lead(group, toks, attn_width),
        out_shape=jax.ShapeDtypeStruct((query_heads, toks, attn_width), BF16),
        compiler_params=params,
        cost_estimate=pl.CostEstimate(flops=4 * 10**9, bytes_accessed=4 * 10**6, transcendentals=10**6),
        name="attention",
    )(heads_first(attn_query), mask, heads_first(attn_gate), *kv_runs)

    half = heads // 2
    pair_map, pair_off, pair_send = pl.pallas_call(
        compose_kernel,
        grid=(2,),
        in_specs=[lead(half, width, 2 * width)] * 2,
        out_specs=[lead(half, width, width)] * 3,
        out_shape=[
            jax.ShapeDtypeStruct((heads, width, width), BF16),
            jax.ShapeDtypeStruct((heads, width, width), F32),
            jax.ShapeDtypeStruct((heads, width, width), BF16),
        ],
        compiler_params=params,
        name="compose",
    )(near, far)
    behind = shifted(pair_send, 2)
    delta_out = pl.pallas_call(
        output_kernel,
        grid=(2,),
        in_specs=[lead(half, toks, width)] * 2 + [lead(half, width, width)] * 3 + [lead(half, toks, width)],
        out_specs=lead(half, toks, width),
        out_shape=jax.ShapeDtypeStruct((heads, toks, width), BF16),
        compiler_params=params,
        name="delta_output",
    )(base, read, pair_map, pair_off, behind, heads_first(output_gate))
    return heads_first(delta_out), heads_first(attended)


def solution(mesh):
    tok = P(("groups", "seq"), None, None)
    flat = P(("groups", "seq"), None)
    return jax.shard_map(
        local,
        mesh=mesh,
        in_specs=(tok, tok, tok, flat, flat, tok, tok, tok, tok, tok, P("groups")),
        out_specs=(tok, tok),
        check_vma=False,
    )
```

time: 447 us -> 96.7 us (0.22)
  the two profiles are of different devices: /device:TPU:29 before, /device:TPU:8 now
where the time goes in v1:
time: 96.7 us; the launch traced here: 95 us
  waiting for transfers between devices  43.8 us (45%)
  starting transfers between devices  19.8 us (20%)
  Pallas kernels  19.6 us (20%)
  local copies, waits for them, and re-layouts  8.47 us (9%)
  other arithmetic  2.31 us (2%)
  between operations  1.05 us (1%)
    ppermute x7, waiting for transfers between devices, shifted(): return lax.ppermute(block, 'seq', route)  43.8 us
    ppermute x7, starting transfers between devices, shifted(): return lax.ppermute(block, 'seq', route)  19.8 us
    pallas_call x1, Pallas kernels, local(): pl.pallas_call(functools.partial(chunk_kernel, per, ratio), grid=(steps,)...  14.6 us
    unnamed x26, local copies, waits for them, and re-layouts  5.35 us
    pallas_call x1, Pallas kernels, local(): pl.pallas_call(functools.partial(attention_kernel, attn_width ** (-0.5),...  3.33 us
  transfers between devices with their start and end apart: 7, of which 5 were waited for; matrix products, arithmetic and copies ran while one was open for 2% of the time, Pallas kernels for 4%

profile of v1, /device:TPU:8, one launch (start us, length us, event | category | flops | bytes accessed | tf_op | source)
XLA Modules:
  0.0 95.0 jit_solution(11123079894684620770)
XLA Ops:
  0.6 0.8 pad_dynamic-slice_fusion
  1.5 0.6 slice.21
  2.1 0.8 copy.104
  2.9 0.2 reduce_window_sum.11
  3.1 0.2 multiply_reduce_fusion.1
  3.4 0.6 copy-done.1
  4.1 0.2 multiply_reduce_fusion
  4.3 0.7 copy-done.2
  5.0 0.1 copy.129
  5.4 0.6 slice.23
  6.1 1.3 %compare_convert_fusion = (f32[128]{0:T(128)S(1)}, f32[128]{0:T(128)S(1)}) fusion(s32[128]{0:T(128)S(1)} %slice.20, s32[]{:T(128)} %bitcast.8, s32[]{:T(128)} %bitcast.6), kind=kLoop, calls=%fused_computation.30 | loop fusion | flops 512 | bytes 1544 | tf_op jit(solution)/shard_map/convert_element_type | solution.py:160
  7.5 0.7 copy-done.8
  8.9 14.6 %delta_chunk.1 = (bf16[16,128,256]{2,1,0:T(8,128)(2,1)S(1)}, f32[16,128,128]{2,1,0:T(8,128)S(1)}, bf16[16,128,128]{2,1,0:T(8,128)(2,1)S(1)}) custom-call(bf16[8,128,128]{2,1,0:T(8,128)(2,1)S(1)} %get-tuple-element.29.q_ref, bf16[8,128,128]{2,1,0:T(8,128)(2,1)S(1)} %get-tuple-element.28.k_ref, bf16[16,128,128]{2,1,0:T(8,128)(2,1)S(1)} %bitcast.48, ...), custom_call_target="tpu_custom_call" | custom-call | flops 4000000000 | bytes 4000000 | tf_op jit(solution)/shard_map/delta_chunk/pallas_call | solution.py:184
  23.5 2.1 %collective-permute-start = (bf16[16,128,256]{2,1,0:T(8,128)(2,1)S(1)}, bf16[16,128,256]{2,1,0:T(8,128)(2,1)S(1)}, u32[]{:S(2)}, u32[]{:S(2)}) collective-permute-start(bf16[16,128,256]{2,1,0:T(8,128)(2,1)S(1)} %get-tuple-element.10), channel_id=1, source_target_pairs={{0,1},{1,2},{2,3},{3,4},{4,5},{5,6},{6,7},{7,8},{8,9},{9,10},{10,1... | collective-permute-start | bytes 3145736 | tf_op jit(solution)/shard_map/ppermute | solution.py:38
  25.5 3.4 %collective-permute-start.1 = (bf16[16,128,256]{2,1,0:T(8,128)(2,1)S(1)}, bf16[16,128,256]{2,1,0:T(8,128)(2,1)S(1)}, u32[]{:S(2)}, u32[]{:S(2)}) collective-permute-start(bf16[16,128,256]{2,1,0:T(8,128)(2,1)S(1)} %get-tuple-element.10), channel_id=1, source_target_pairs={{0,2},{1,3},{2,4},{3,5},{4,6},{5,7},{6,8},{7,9},{8,10},{9,11},{10,... | collective-permute-start | bytes 3145736 | tf_op jit(solution)/shard_map/ppermute | solution.py:38
  29.1 3.6 %collective-permute-start.3 = (bf16[2,2,128,256]{3,2,1,0:T(8,128)(2,1)S(1)}, bf16[2,2,128,256]{3,2,1,0:T(8,128)(2,1)S(1)}, u32[]{:S(2)}, u32[]{:S(2)}) collective-permute-start(bf16[2,2,128,256]{3,2,1,0:T(8,128)(2,1)S(1)} %pad_maximum_fusion.refs_4_), channel_id=1, source_target_pairs={{0,4},{1,5},{2,6},{3,7},{4,8},{5,9},{6,10},{7,11},{8,12},{9,13},{1... | collective-permute-start | bytes 786440 | tf_op jit(solution)/shard_map/ppermute | solution.py:38
  32.7 4.1 %collective-permute-start.4 = (bf16[2,2,128,256]{3,2,1,0:T(8,128)(2,1)S(1)}, bf16[2,2,128,256]{3,2,1,0:T(8,128)(2,1)S(1)}, u32[]{:S(2)}, u32[]{:S(2)}) collective-permute-start(bf16[2,2,128,256]{3,2,1,0:T(8,128)(2,1)S(1)} %pad_maximum_fusion.refs_4_), channel_id=1, source_target_pairs={{0,3},{1,4},{2,5},{3,6},{4,7},{5,8},{6,9},{7,10},{8,11},{9,12},{10... | collective-permute-start | bytes 786440 | tf_op jit(solution)/shard_map/ppermute | solution.py:38
  36.8 2.2 %collective-permute-start.5 = (bf16[2,2,128,256]{3,2,1,0:T(8,128)(2,1)S(1)}, bf16[2,2,128,256]{3,2,1,0:T(8,128)(2,1)S(1)}, u32[]{:S(2)}, u32[]{:S(2)}) collective-permute-start(bf16[2,2,128,256]{3,2,1,0:T(8,128)(2,1)S(1)} %pad_maximum_fusion.refs_4_), channel_id=1, source_target_pairs={{0,2},{1,3},{2,4},{3,5},{4,6},{5,7},{6,8},{7,9},{8,10},{9,11},{10,... | collective-permute-start | bytes 786440 | tf_op jit(solution)/shard_map/ppermute | solution.py:38
  39.0 10.3 %collective-permute-done.near_ref = bf16[16,128,256]{2,1,0:T(8,128)(2,1)S(1)} collective-permute-done((bf16[16,128,256]{2,1,0:T(8,128)(2,1)S(1)}, bf16[16,128,256]{2,1,0:T(8,128)(2,1)S(1)}, u32[]{:S(2)}, u32[]{:S(2)}) %collective-permute-start) | collective-permute-done | bytes 1048608 | tf_op jit(solution)/shard_map/ppermute | solution.py:38
  49.3 1.9 %collective-permute-start.6 = (bf16[2,2,128,256]{3,2,1,0:T(8,128)(2,1)S(1)}, bf16[2,2,128,256]{3,2,1,0:T(8,128)(2,1)S(1)}, u32[]{:S(2)}, u32[]{:S(2)}) collective-permute-start(bf16[2,2,128,256]{3,2,1,0:T(8,128)(2,1)S(1)} %pad_maximum_fusion.refs_4_), channel_id=1, source_target_pairs={{0,1},{1,2},{2,3},{3,4},{4,5},{5,6},{6,7},{7,8},{8,9},{9,10},{10,1... | collective-permute-start | bytes 786440 | tf_op jit(solution)/shard_map/ppermute | solution.py:38
  51.2 0.2 copy_bitcast_fusion
  51.4 0.1 copy.128
  51.6 2.8 %collective-permute-done.1.far_ref = bf16[16,128,256]{2,1,0:T(8,128)(2,1)S(1)} collective-permute-done((bf16[16,128,256]{2,1,0:T(8,128)(2,1)S(1)}, bf16[16,128,256]{2,1,0:T(8,128)(2,1)S(1)}, u32[]{:S(2)}, u32[]{:S(2)}) %collective-permute-start.1) | collective-permute-done | bytes 1048608 | tf_op jit(solution)/shard_map/ppermute | solution.py:38
  54.4 0.6 compose.1
  55.0 2.5 %collective-permute-start.2 = (bf16[16,128,128]{2,1,0:T(8,128)(2,1)S(1)}, bf16[16,128,128]{2,1,0:T(8,128)(2,1)S(1)}, u32[]{:S(2)}, u32[]{:S(2)}) collective-permute-start(bf16[16,128,128]{2,1,0:T(8,128)(2,1)S(1)} %get-tuple-element.13), channel_id=1, source_target_pairs={{0,2},{1,3},{2,4},{3,5},{4,6},{5,7},{6,8},{7,9},{8,10},{9,11},{10,... | collective-permute-start | bytes 1572872 | tf_op jit(solution)/shard_map/ppermute | solution.py:38
  57.7 0.5 collective-permute-done.4.refs_1_
  58.2 13.1 %collective-permute-done.5.refs_2_ = bf16[2,2,128,256]{3,2,1,0:T(8,128)(2,1)S(1)} collective-permute-done((bf16[2,2,128,256]{3,2,1,0:T(8,128)(2,1)S(1)}, bf16[2,2,128,256]{3,2,1,0:T(8,128)(2,1)S(1)}, u32[]{:S(2)}, u32[]{:S(2)}) %collective-permute-start.5) | collective-permute-done | bytes 262176 | tf_op jit(solution)/shard_map/ppermute | solution.py:38
  71.3 17.1 %collective-permute-done.6.refs_3_ = bf16[2,2,128,256]{3,2,1,0:T(8,128)(2,1)S(1)} collective-permute-done((bf16[2,2,128,256]{3,2,1,0:T(8,128)(2,1)S(1)}, bf16[2,2,128,256]{3,2,1,0:T(8,128)(2,1)S(1)}, u32[]{:S(2)}, u32[]{:S(2)}) %collective-permute-start.6) | collective-permute-done | bytes 262176 | tf_op jit(solution)/shard_map/ppermute | solution.py:38
  88.3 3.3 %attention.1 = bf16[8,128,256]{2,1,0:T(8,128)(2,1)S(1)} custom-call(bf16[8,128,256]{2,1,0:T(8,128)(2,1)S(1)} %get-tuple-element.33.q_ref, f32[128,640]{1,0:T(8,128)S(1)} %broadcast_select_fusion.mask_ref, bf16[8,128,256]{2,1,0:T(8,128)(2,1)S(1)} %get-tuple-element.32.gate_ref, bf16[2,2,128,256]{3,2,1,0:T(8,128)(2,1)S(1)} %collective-permute-done.3.refs_0_, ...), custom_call_target="tpu_custom_call" | custom-call | flops 4000000000 | bytes 4000000 | tf_op jit(solution)/shard_map/attention/pallas_call | solution.py:209
  91.7 1.1 %copy.119 = bf16[128,8,256]{2,1,0:T(8,128)(2,1)} copy(bf16[128,8,256]{2,0,1:T(8,128)(2,1)S(1)} %bitcast.49) | data formatting | bytes 1048576
  92.8 1.1 %delta_output.1 = bf16[16,128,128]{2,1,0:T(8,128)(2,1)S(1)} custom-call(f32[16,128,128]{2,1,0:T(8,128)S(1)} %get-tuple-element.8.base_ref, bf16[16,128,128]{2,1,0:T(8,128)(2,1)S(1)} %get-tuple-element.9.read_ref, bf16[16,128,128]{2,1,0:T(8,128)(2,1)S(1)} %get-tuple-element.11.map_ref, f32[16,128,128]{2,1,0:T(8,128)S(1)} %get-tuple-element.12.off_ref, ...), custom_call_target="tpu_custom_call" | custom-call | tf_op jit(solution)/shard_map/delta_output/pallas_call | solution.py:240
  93.9 1.1 %copy.118 = bf16[128,16,128]{2,1,0:T(8,128)(2,1)} copy(bf16[128,16,128]{2,0,1:T(8,128)(2,1)S(1)} %bitcast.47) | data formatting | bytes 1048576
  (53 shorter events, 1.4 us)
Async XLA Ops:
  0.6 2.5 %copy-start = (bf16[128,8,128]{2,1,0:T(8,128)(2,1)S(1)}, bf16[128,8,128]{2,1,0:T(8,128)(2,1)}, u32[]{:S(2)}) copy-start(bf16[128,8,128]{2,1,0:T(8,128)(2,1)} %param.12) | copy-start | bytes 786436
  3.0 1.0 %copy-start.1 = (bf16[128,8,128]{2,1,0:T(8,128)(2,1)S(1)}, bf16[128,8,128]{2,1,0:T(8,128)(2,1)}, u32[]{:S(2)}) copy-start(bf16[128,8,128]{2,1,0:T(8,128)(2,1)} %param.11) | copy-start | bytes 786436
  4.0 1.0 %copy-start.2 = (bf16[128,16,128]{2,1,0:T(8,128)(2,1)S(1)}, bf16[128,16,128]{2,1,0:T(8,128)(2,1)}, u32[]{:S(2)}) copy-start(bf16[128,16,128]{2,1,0:T(8,128)(2,1)} %param.13) | copy-start | bytes 1572868
  7.5 0.7 copy-start.8
  8.8 20.1 %copy-start.6 = (bf16[128,2,256]{2,1,0:T(2,128)(2,1)S(1)}, bf16[128,2,256]{2,1,0:T(2,128)(2,1)}, u32[]{:S(2)}) copy-start(bf16[128,2,256]{2,1,0:T(2,128)(2,1)} %param.19) | copy-start | bytes 393220
  8.9 20.1 %copy-start.7 = (bf16[128,2,256]{2,1,0:T(2,128)(2,1)S(1)}, bf16[128,2,256]{2,1,0:T(2,128)(2,1)}, u32[]{:S(2)}) copy-start(bf16[128,2,256]{2,1,0:T(2,128)(2,1)} %param.18) | copy-start | bytes 393220
  23.4 27.8 %copy-start.4 = (bf16[128,8,256]{2,1,0:T(8,128)(2,1)S(1)}, bf16[128,8,256]{2,1,0:T(8,128)(2,1)}, u32[]{:S(2)}) copy-start(bf16[128,8,256]{2,1,0:T(8,128)(2,1)} %param.20) | copy-start | bytes 1572868
  23.4 27.8 %copy-start.5 = (bf16[128,8,256]{2,1,0:T(8,128)(2,1)S(1)}, bf16[128,8,256]{2,1,0:T(8,128)(2,1)}, u32[]{:S(2)}) copy-start(bf16[128,8,256]{2,1,0:T(8,128)(2,1)} %param.17) | copy-start | bytes 1572868
  23.5 25.8 %collective-permute-start = (bf16[16,128,256]{2,1,0:T(8,128)(2,1)S(1)}, bf16[16,128,256]{2,1,0:T(8,128)(2,1)S(1)}, u32[]{:S(2)}, u32[]{:S(2)}) collective-permute-start(bf16[16,128,256]{2,1,0:T(8,128)(2,1)S(1)} %get-tuple-element.10), channel_id=1, source_target_pairs={{0,1},{1,2},{2,3},{3,4},{4,5},{5,6},{6,7},{7,8},{8,9},{9,10},{10,1... | collective-permute-start | bytes 3145736 | tf_op jit(solution)/shard_map/ppermute | solution.py:38
  25.5 28.9 %collective-permute-start.1 = (bf16[16,128,256]{2,1,0:T(8,128)(2,1)S(1)}, bf16[16,128,256]{2,1,0:T(8,128)(2,1)S(1)}, u32[]{:S(2)}, u32[]{:S(2)}) collective-permute-start(bf16[16,128,256]{2,1,0:T(8,128)(2,1)S(1)} %get-tuple-element.10), channel_id=1, source_target_pairs={{0,2},{1,3},{2,4},{3,5},{4,6},{5,7},{6,8},{7,9},{8,10},{9,11},{10,... | collective-permute-start | bytes 3145736 | tf_op jit(solution)/shard_map/ppermute | solution.py:38
  29.1 22.4 %copy-start.3 = (bf16[128,16,128]{2,1,0:T(8,128)(2,1)S(1)}, bf16[128,16,128]{2,1,0:T(8,128)(2,1)}, u32[]{:S(2)}) copy-start(bf16[128,16,128]{2,1,0:T(8,128)(2,1)} %param.16) | copy-start | bytes 1572868
  29.1 28.6 %collective-permute-start.3 = (bf16[2,2,128,256]{3,2,1,0:T(8,128)(2,1)S(1)}, bf16[2,2,128,256]{3,2,1,0:T(8,128)(2,1)S(1)}, u32[]{:S(2)}, u32[]{:S(2)}) collective-permute-start(bf16[2,2,128,256]{3,2,1,0:T(8,128)(2,1)S(1)} %pad_maximum_fusion.refs_4_), channel_id=1, source_target_pairs={{0,4},{1,5},{2,6},{3,7},{4,8},{5,9},{6,10},{7,11},{8,12},{9,13},{1... | collective-permute-start | bytes 786440 | tf_op jit(solution)/shard_map/ppermute | solution.py:38
  32.7 25.5 %collective-permute-start.4 = (bf16[2,2,128,256]{3,2,1,0:T(8,128)(2,1)S(1)}, bf16[2,2,128,256]{3,2,1,0:T(8,128)(2,1)S(1)}, u32[]{:S(2)}, u32[]{:S(2)}) collective-permute-start(bf16[2,2,128,256]{3,2,1,0:T(8,128)(2,1)S(1)} %pad_maximum_fusion.refs_4_), channel_id=1, source_target_pairs={{0,3},{1,4},{2,5},{3,6},{4,7},{5,8},{6,9},{7,10},{8,11},{9,12},{10... | collective-permute-start | bytes 786440 | tf_op jit(solution)/shard_map/ppermute | solution.py:38
  36.8 34.5 %collective-permute-start.5 = (bf16[2,2,128,256]{3,2,1,0:T(8,128)(2,1)S(1)}, bf16[2,2,128,256]{3,2,1,0:T(8,128)(2,1)S(1)}, u32[]{:S(2)}, u32[]{:S(2)}) collective-permute-start(bf16[2,2,128,256]{3,2,1,0:T(8,128)(2,1)S(1)} %pad_maximum_fusion.refs_4_), channel_id=1, source_target_pairs={{0,2},{1,3},{2,4},{3,5},{4,6},{5,7},{6,8},{7,9},{8,10},{9,11},{10,... | collective-permute-start | bytes 786440 | tf_op jit(solution)/shard_map/ppermute | solution.py:38
  49.3 39.1 %collective-permute-start.6 = (bf16[2,2,128,256]{3,2,1,0:T(8,128)(2,1)S(1)}, bf16[2,2,128,256]{3,2,1,0:T(8,128)(2,1)S(1)}, u32[]{:S(2)}, u32[]{:S(2)}) collective-permute-start(bf16[2,2,128,256]{3,2,1,0:T(8,128)(2,1)S(1)} %pad_maximum_fusion.refs_4_), channel_id=1, source_target_pairs={{0,1},{1,2},{2,3},{3,4},{4,5},{5,6},{6,7},{7,8},{8,9},{9,10},{10,1... | collective-permute-start | bytes 786440 | tf_op jit(solution)/shard_map/ppermute | solution.py:38
  55.0 37.8 %collective-permute-start.2 = (bf16[16,128,128]{2,1,0:T(8,128)(2,1)S(1)}, bf16[16,128,128]{2,1,0:T(8,128)(2,1)S(1)}, u32[]{:S(2)}, u32[]{:S(2)}) collective-permute-start(bf16[16,128,128]{2,1,0:T(8,128)(2,1)S(1)} %get-tuple-element.13), channel_id=1, source_target_pairs={{0,2},{1,3},{2,4},{3,5},{4,6},{5,7},{6,8},{7,9},{8,10},{9,11},{10,... | collective-permute-start | bytes 1572872 | tf_op jit(solution)/shard_map/ppermute | solution.py:38

commit v2 on v1

v2 whole, which is shorter than its diff:
```python
import functools

import jax
import jax.numpy as jnp
from jax import lax
from jax.experimental import pallas as pl
from jax.experimental.pallas import tpu as pltpu
from jax.sharding import PartitionSpec as P

BLK = 64
SPAN = 4
F32 = jnp.float32
BF16 = jnp.bfloat16
MESH = pl.DeviceIdType.MESH


def mm(a, b):
    return jnp.dot(a, b, preferred_element_type=F32)


def mm_nt(a, b):
    return lax.dot_general(a, b, (((1,), (1,)), ((), ())), preferred_element_type=F32)


def split(x):
    high = x.astype(BF16)
    return high, (x - high.astype(F32)).astype(BF16)


def mm3(a, b):
    ah, al = a
    bh, bl = b
    return mm(ah, bh) + (mm(ah, bl) + mm(al, bh))


def chunk_step(i, heads, ratio, q_ref, k_ref, v_ref, col_ref, row_ref, incl_ref, map_ref, off_ref, base_ref, read_ref, send_ref):
    length = k_ref.shape[1]
    pairs = heads // ratio
    col, row = col_ref[i], row_ref[i]
    incl = incl_ref[...] > 0
    rows = lax.broadcasted_iota(jnp.int32, (length, length), 0)
    cols = lax.broadcasted_iota(jnp.int32, (length, length), 1)
    eye = (rows == cols).astype(F32)
    grams = []
    for j in range(heads // ratio):
        k = k_ref[i * pairs + j]
        grams.append((mm_nt(k, k), mm_nt(q_ref[i * pairs + j], k), k.T))
    decays, lows = [], []
    for h in range(heads):
        c_col, rk_col = col[:, 5 * h : 5 * h + 1], col[:, 5 * h + 1 : 5 * h + 2]
        c_row, bk_row = row[3 * h : 3 * h + 1], row[3 * h + 1 : 3 * h + 2]
        decay = jnp.exp(jnp.where(incl, c_col - c_row, -1e30)) * bk_row
        decays.append(decay)
        lows.append(jnp.where(rows > cols, decay * rk_col * grams[h // ratio][0], 0.0))
    inverses = [eye - jnp.where(rows // 2 == cols // 2, low, 0.0) for low in lows]
    size = 2
    while size < length:
        band = (rows // (2 * size) == cols // (2 * size)) & (rows // size != cols // size)
        parts = [split(x) for x in inverses]
        tops = [mm3(split(jnp.where(band, low, 0.0)), x) for low, x in zip(lows, parts)]
        inverses = [x - mm3(xp, split(t)) for x, xp, t in zip(inverses, parts, tops)]
        size *= 2
    for h in range(heads):
        k_gram, q_gram, k_t = grams[h // ratio]
        k, q, v = k_ref[i * pairs + h // ratio], q_ref[i * pairs + h // ratio], v_ref[i * heads + h]
        rq_col, gq_col, tk_col = (col[:, 5 * h + n : 5 * h + n + 1] for n in (2, 3, 4))
        gain = col[length - 1 : length, 5 * heads + h : 5 * heads + h + 1]
        gk_row = row[3 * h + 2 : 3 * h + 3]
        th, tl = split(inverses[h])
        update = mm(th, v) + mm(tl, v)
        wh, wl = split(inverses[h] * gk_row)
        write = mm(wh, k) + mm(wl, k)
        both = jnp.concatenate([write, update], axis=1)
        th, tl = split(both * tk_col)
        tail = mm(k_t, th) + mm(k_t, tl)
        map_ref[i, h] = (eye * gain - tail[:, :length]).astype(BF16)
        off_ref[i, h] = tail[:, length:]
        send_ref[0, i, h] = tail[:, length:].astype(BF16)
        mix = (decays[h] * rq_col * q_gram).astype(BF16)
        mixed = mm(mix, both.astype(BF16))
        base_ref[i, h] = mixed[:, length:]
        read_ref[i, h] = (gq_col * q.astype(F32) - mixed[:, :length]).astype(BF16)


def layer_kernel(
    per,
    ratio,
    scale,
    q_ref,
    k_ref,
    v_ref,
    col_ref,
    row_ref,
    incl_ref,
    gate_ref,
    kv_ref,
    aq_ref,
    mask_ref,
    agate_ref,
    out_ref,
    att_ref,
    kv_in,
    map_ref,
    off_ref,
    base_ref,
    read_ref,
    send_ref,
    recv_ref,
    kv_send_sem,
    kv_recv_sem,
    send_sem,
    recv_sem,
):
    size = lax.axis_size("seq")
    me = lax.axis_index("seq")
    steps = map_ref.shape[0]

    def device(d):
        return {"seq": lax.rem(me + d + size, size)}

    barrier = pltpu.get_barrier_semaphore()
    for d in range(1, SPAN + 1):
        for side in (d, -d):
            pl.semaphore_signal(barrier, inc=1, device_id=device(side), device_id_type=MESH)
    pl.semaphore_wait(barrier, 2 * SPAN)

    def kv_copy(d):
        return pltpu.make_async_remote_copy(
            src_ref=kv_ref,
            dst_ref=kv_in.at[d - 1],
            send_sem=kv_send_sem.at[d - 1],
            recv_sem=kv_recv_sem.at[d - 1],
            device_id=device(d),
            device_id_type=MESH,
        )

    def hop_copy(hop, i):
        return pltpu.make_async_remote_copy(
            src_ref=send_ref.at[hop, i],
            dst_ref=recv_ref.at[hop, i],
            send_sem=send_sem.at[hop, i],
            recv_sem=recv_sem.at[hop, i],
            device_id=device(1),
            device_id_type=MESH,
        )

    for d in range(1, SPAN + 1):
        kv_copy(d).start()

    @pl.loop(0, steps)
    def _(i):
        chunk_step(
            i, per, ratio, q_ref, k_ref, v_ref, col_ref, row_ref, incl_ref, map_ref, off_ref, base_ref, read_ref, send_ref
        )
        hop_copy(0, i).start()

    for d in range(1, SPAN + 1):
        kv_copy(d).wait_recv()
    group = aq_ref.shape[0] // kv_ref.shape[1]

    @pl.loop(0, kv_ref.shape[1])
    def _(g):
        keys = jnp.concatenate([kv_in[d - 1, 0, g] for d in range(SPAN, 0, -1)] + [kv_ref[0, g]], axis=0)
        values = jnp.concatenate([kv_in[d - 1, 1, g] for d in range(SPAN, 0, -1)] + [kv_ref[1, g]], axis=0)
        for j in range(group):
            scores = mm_nt(aq_ref[g * group + j], keys) * scale + mask_ref[...]
            weights = jnp.exp(scores - jnp.max(scores, axis=-1, keepdims=True))
            total = jnp.sum(weights, axis=-1, keepdims=True)
            mixed = mm(weights.astype(BF16), values)
            gate = agate_ref[g * group + j].astype(F32)
            att_ref[g * group + j] = (mixed / total / (1.0 + jnp.exp(-gate))).astype(BF16)

    @pl.loop(0, (SPAN - 1) * steps)
    def _(r):
        hop, i = r // steps, r % steps
        hop_copy(hop, i).wait_recv()
        for h in range(per):
            state = mm(map_ref[i, h], recv_ref[hop, i, h]) + off_ref[i, h]
            send_ref[hop + 1, i, h] = state.astype(BF16)
        hop_copy(hop + 1, i).start()

    @pl.loop(0, steps)
    def _(i):
        hop_copy(SPAN - 1, i).wait_recv()
        for h in range(per):
            core = base_ref[i, h] + mm(read_ref[i, h], recv_ref[SPAN - 1, i, h])
            factor = lax.rsqrt(jnp.mean(core * core, axis=-1, keepdims=True) + 1e-06)
            gate = gate_ref[i * per + h].astype(F32)
            out_ref[i * per + h] = (core * factor * (gate / (1.0 + jnp.exp(-gate)))).astype(BF16)

    for d in range(1, SPAN + 1):
        kv_copy(d).wait_send()

    @pl.loop(0, SPAN * steps)
    def _(r):
        hop_copy(r // steps, r % steps).wait_send()


def local(
    delta_query,
    delta_key,
    delta_value,
    log_decay,
    write_logit,
    output_gate,
    attn_query,
    attn_key,
    attn_value,
    attn_gate,
    doc_ids,
):
    position = lax.axis_index("seq")
    toks, key_heads, width = delta_key.shape
    heads = delta_value.shape[1]
    ratio = heads // key_heads
    blocks = toks // BLK
    kv_heads, attn_width = attn_key.shape[1:]
    query_heads = attn_query.shape[1]
    group = query_heads // kv_heads
    runs = SPAN + 1

    def heads_first(x):
        return x.transpose(1, 0, 2)

    kv = jnp.stack([heads_first(attn_key), heads_first(attn_value)])

    padded = jnp.concatenate([jnp.full((SPAN * blocks,), -1, doc_ids.dtype), doc_ids])
    window = lax.dynamic_slice_in_dim(padded, position * blocks, runs * blocks)
    key_doc = jnp.repeat(window, BLK)
    tok_doc = key_doc[SPAN * toks :]
    t = jnp.arange(toks, dtype=jnp.int32)
    key_pos = jnp.arange(runs * toks, dtype=jnp.int32) - SPAN * toks
    allowed = (key_doc[None, :] == tok_doc[:, None]) & (key_pos[None, :] <= t[:, None])
    mask = jnp.where(allowed, 0.0, -1e30).astype(F32)
    incl = allowed[:, SPAN * toks :].astype(F32)
    carried = (tok_doc == window[SPAN * blocks - 1]).astype(F32)[:, None]
    lasting = (tok_doc == tok_doc[-1]).astype(F32)[:, None]

    def unit_factor(x):
        x = x.astype(F32)
        return jnp.repeat(lax.rsqrt(jnp.sum(x * x, axis=-1) + 1e-06), ratio, axis=1)

    cum = jnp.cumsum(log_decay, axis=0)
    writes = jax.nn.sigmoid(write_logit)
    rq, rk = unit_factor(delta_query), unit_factor(delta_key)
    grown = jnp.exp(cum) * carried
    tail = jnp.exp(cum[-1:] - cum) * writes * lasting
    per = 4
    steps = heads // per
    cols = jnp.stack([cum, rk, rq, grown * rq, tail * rk], axis=-1)
    cols = cols.reshape(toks, steps, per * 5)
    cols = jnp.concatenate([cols, grown.reshape(toks, steps, per)], axis=-1).transpose(1, 0, 2)
    rowv = jnp.stack([cum, writes * rk, grown * rk], axis=-1)
    rowv = rowv.reshape(toks, steps, per * 3).transpose(1, 2, 0)

    delta_out, attended = pl.pallas_call(
        functools.partial(layer_kernel, per, ratio, attn_width ** (-0.5)),
        in_specs=[pl.BlockSpec(memory_space=pltpu.VMEM)] * 11,
        out_specs=[pl.BlockSpec(memory_space=pltpu.VMEM)] * 2,
        out_shape=[
            jax.ShapeDtypeStruct((heads, toks, width), BF16),
            jax.ShapeDtypeStruct((query_heads, toks, attn_width), BF16),
        ],
        scratch_shapes=[
            pltpu.VMEM((SPAN, 2, kv_heads, toks, attn_width), BF16),
            pltpu.VMEM((steps, per, width, width), BF16),
            pltpu.VMEM((steps, per, width, width), F32),
            pltpu.VMEM((steps, per, toks, width), F32),
            pltpu.VMEM((steps, per, toks, width), BF16),
            pltpu.VMEM((SPAN, steps, per, width, width), BF16),
            pltpu.VMEM((SPAN, steps, per, width, width), BF16),
            pltpu.SemaphoreType.DMA((SPAN,)),
            pltpu.SemaphoreType.DMA((SPAN,)),
            pltpu.SemaphoreType.DMA((SPAN, steps)),
            pltpu.SemaphoreType.DMA((SPAN, steps)),
        ],
        compiler_params=pltpu.CompilerParams(
            collective_id=0, has_side_effects=True, vmem_limit_bytes=48 * 1024 * 1024
        ),
        cost_estimate=pl.CostEstimate(flops=8 * 10**9, bytes_accessed=8 * 10**6, transcendentals=2 * 10**6),
        name="layer",
    )(
        heads_first(delta_query),
        heads_first(delta_key),
        heads_first(delta_value),
        cols,
        rowv,
        incl,
        heads_first(output_gate),
        kv,
        heads_first(attn_query),
        mask,
        heads_first(attn_gate),
    )
    return heads_first(delta_out), heads_first(attended)


def solution(mesh):
    tok = P(("groups", "seq"), None, None)
    flat = P(("groups", "seq"), None)
    return jax.shard_map(
        local,
        mesh=mesh,
        in_specs=(tok, tok, tok, flat, flat, tok, tok, tok, tok, tok, P("groups")),
        out_specs=(tok, tok),
        check_vma=False,
    )
```

time: 96.7 us -> 64.7 us (0.67)
  the two profiles are of different devices: /device:TPU:8 before, /device:TPU:0 now
where the time goes in v2:
time: 64.7 us; the launch traced here: 64.4 us
  Pallas kernels  50.8 us (79%)
  local copies, waits for them, and re-layouts  10.4 us (16%)
  other arithmetic  2.26 us (3%)
  between operations  0.88 us (1%)
    pallas_call x1, Pallas kernels, local(): pl.pallas_call(functools.partial(layer_kernel, per, ratio, attn_width **...  50.8 us
    unnamed x28, local copies, waits for them, and re-layouts  7.76 us

profile of v2, /device:TPU:0, one launch (start us, length us, event | category | flops | bytes accessed | tf_op | source)
XLA Modules:
  0.0 64.4 jit_solution(11563452503847044293)
XLA Ops:
  0.6 0.6 %copy-done.10 = s32[32]{0:T(128)S(1)} copy-done((s32[32]{0:T(128)S(1)}, s32[32]{0:T(128)}, u32[]{:S(2)}) %copy-start.10) | copy-done | bytes 152
  1.3 0.1 pad_dynamic-slice_fusion
  1.4 0.6 slice.21
  2.0 0.1 slice.19
  2.0 0.1 broadcast_in_dim.26
  2.1 0.1 slice.20
  2.2 0.6 slice.23
  2.8 1.3 %compare_convert_fusion = (f32[128]{0:T(128)S(1)}, f32[128]{0:T(128)S(1)}) fusion(s32[128]{0:T(128)S(1)} %slice.20, s32[]{:T(128)} %bitcast.8, s32[]{:T(128)} %bitcast.6), kind=kLoop, calls=%fused_computation.30 | loop fusion | flops 512 | bytes 1544 | tf_op jit(solution)/shard_map/convert_element_type | solution.py:237
  4.1 0.1 broadcast_in_dim.27
  4.2 0.6 copy-done.9
  4.9 0.1 copy.104
  5.0 0.2 reduce_window_sum.11
  5.3 0.5 copy-done.1
  5.8 0.2 multiply_reduce_fusion
  6.1 0.1 copy-done
  6.2 0.2 multiply_reduce_fusion.1
  6.5 0.7 %copy-done.8 = f32[128,16]{0,1:T(8,128)S(1)} copy-done((f32[128,16]{0,1:T(8,128)S(1)}, f32[128,16]{0,1:T(8,128)}, u32[]{:S(2)}) %copy-start.8) | copy-done | bytes 8216
  7.2 0.1 constant_dynamic-update-slice_fusion
  7.4 0.1 fusion
  7.6 0.1 copy.111
  7.7 0.8 %copy-done.6 = bf16[128,2,256]{2,1,0:T(2,128)(2,1)S(1)} copy-done((bf16[128,2,256]{2,1,0:T(2,128)(2,1)S(1)}, bf16[128,2,256]{2,1,0:T(2,128)(2,1)}, u32[]{:S(2)}) %copy-start.6) | copy-done | bytes 131096
  8.6 0.1 broadcast_select_fusion.mask_ref
  8.7 0.1 copy_bitcast_fusion.4
  8.8 0.9 %copy-done.2 = bf16[128,16,128]{2,1,0:T(8,128)(2,1)S(1)} copy-done((bf16[128,16,128]{2,1,0:T(8,128)(2,1)S(1)}, bf16[128,16,128]{2,1,0:T(8,128)(2,1)}, u32[]{:S(2)}) %copy-start.2) | copy-done | bytes 524312
  9.7 0.2 copy-done.3
  9.9 0.3 copy_bitcast_fusion.2
  10.2 0.8 %copy-done.4 = bf16[128,8,256]{2,1,0:T(8,128)(2,1)S(1)} copy-done((bf16[128,8,256]{2,1,0:T(8,128)(2,1)S(1)}, bf16[128,8,256]{2,1,0:T(8,128)(2,1)}, u32[]{:S(2)}) %copy-start.4) | copy-done | bytes 524312
  10.9 0.2 copy-done.5
  11.1 0.2 copy_bitcast_fusion
  11.3 50.8 %layer.1 = (bf16[16,128,128]{2,1,0:T(8,128)(2,1)S(1)}, bf16[8,128,256]{2,1,0:T(8,128)(2,1)S(1)}) custom-call(bf16[8,128,128]{2,1,0:T(8,128)(2,1)S(1)} %get-tuple-element.27.q_ref, bf16[8,128,128]{2,1,0:T(8,128)(2,1)S(1)} %get-tuple-element.26.k_ref, bf16[16,128,128]{2,1,0:T(8,128)(2,1)S(1)} %get-tuple-element.25.v_ref, f32[4,128,24]{2,1,0:T(8,128)S(1)} %bitcast.46, ...), custom_call_target="tpu_custom_call" | custom-call | flops 8000000000 | bytes 8000000 | tf_op jit(solution)/shard_map/layer/pallas_call | solution.py:256
  62.1 1.1 %copy.118 = bf16[128,16,128]{2,1,0:T(8,128)(2,1)} copy(bf16[128,16,128]{2,0,1:T(8,128)(2,1)S(1)} %bitcast.45) | data formatting | bytes 1048576
  63.3 1.1 %copy.119 = bf16[128,8,256]{2,1,0:T(8,128)(2,1)} copy(bf16[128,8,256]{2,0,1:T(8,128)(2,1)S(1)} %bitcast.44) | data formatting | bytes 1048576
  (39 shorter events, 0.6 us)
Async XLA Ops:
  0.6 0.7 %copy-start.10 = (s32[32]{0:T(128)S(1)}, s32[32]{0:T(128)}, u32[]{:S(2)}) copy-start(s32[32]{0:T(128)} %param.21) | copy-start | bytes 388
  4.1 0.7 %copy-start.9 = (f32[128,16]{0,1:T(8,128)S(1)}, f32[128,16]{0,1:T(8,128)}, u32[]{:S(2)}) copy-start(f32[128,16]{0,1:T(8,128)} %param.14) | copy-start | bytes 24580
  4.8 0.9 %copy-start.1 = (bf16[128,8,128]{2,1,0:T(8,128)(2,1)S(1)}, bf16[128,8,128]{2,1,0:T(8,128)(2,1)}, u32[]{:S(2)}) copy-start(bf16[128,8,128]{2,1,0:T(8,128)(2,1)} %param.11) | copy-start | bytes 786436
  5.2 1.0 %copy-start = (bf16[128,8,128]{2,1,0:T(8,128)(2,1)S(1)}, bf16[128,8,128]{2,1,0:T(8,128)(2,1)}, u32[]{:S(2)}) copy-start(bf16[128,8,128]{2,1,0:T(8,128)(2,1)} %param.12) | copy-start | bytes 786436
  6.5 0.7 %copy-start.8 = (f32[128,16]{0,1:T(8,128)S(1)}, f32[128,16]{0,1:T(8,128)}, u32[]{:S(2)}) copy-start(f32[128,16]{0,1:T(8,128)} %param.15) | copy-start | bytes 24580
  7.5 0.9 %copy-start.6 = (bf16[128,2,256]{2,1,0:T(2,128)(2,1)S(1)}, bf16[128,2,256]{2,1,0:T(2,128)(2,1)}, u32[]{:S(2)}) copy-start(bf16[128,2,256]{2,1,0:T(2,128)(2,1)} %param.19) | copy-start | bytes 393220
  7.6 1.0 %copy-start.7 = (bf16[128,2,256]{2,1,0:T(2,128)(2,1)S(1)}, bf16[128,2,256]{2,1,0:T(2,128)(2,1)}, u32[]{:S(2)}) copy-start(bf16[128,2,256]{2,1,0:T(2,128)(2,1)} %param.18) | copy-start | bytes 393220
  8.7 1.0 %copy-start.2 = (bf16[128,16,128]{2,1,0:T(8,128)(2,1)S(1)}, bf16[128,16,128]{2,1,0:T(8,128)(2,1)}, u32[]{:S(2)}) copy-start(bf16[128,16,128]{2,1,0:T(8,128)(2,1)} %param.16) | copy-start | bytes 1572868
  8.7 1.2 %copy-start.3 = (bf16[128,16,128]{2,1,0:T(8,128)(2,1)S(1)}, bf16[128,16,128]{2,1,0:T(8,128)(2,1)}, u32[]{:S(2)}) copy-start(bf16[128,16,128]{2,1,0:T(8,128)(2,1)} %param.13) | copy-start | bytes 1572868
  9.9 1.0 %copy-start.4 = (bf16[128,8,256]{2,1,0:T(8,128)(2,1)S(1)}, bf16[128,8,256]{2,1,0:T(8,128)(2,1)}, u32[]{:S(2)}) copy-start(bf16[128,8,256]{2,1,0:T(8,128)(2,1)} %param.20) | copy-start | bytes 1572868
  9.9 1.2 %copy-start.5 = (bf16[128,8,256]{2,1,0:T(8,128)(2,1)S(1)}, bf16[128,8,256]{2,1,0:T(8,128)(2,1)}, u32[]{:S(2)}) copy-start(bf16[128,8,256]{2,1,0:T(8,128)(2,1)} %param.17) | copy-start | bytes 1572868

commit v3 on v2

--- a/solution.py
+++ b/solution.py
@@ -119,18 +119,23 @@
         return {"seq": lax.rem(me + d + size, size)}
 
     barrier = pltpu.get_barrier_semaphore()
-    for d in range(1, SPAN + 1):
-        for side in (d, -d):
-            pl.semaphore_signal(barrier, inc=1, device_id=device(side), device_id_type=MESH)
-    pl.semaphore_wait(barrier, 2 * SPAN)
-
-    def kv_copy(d):
+    place = lax.rem(me, SPAN)
+
+    def fellow(r):
+        return {"seq": me - place + lax.rem(place + r, SPAN)}
+
+    greeted = [device(d) for d in (1, -1, SPAN, -SPAN)] + [fellow(r) for r in range(1, SPAN)]
+    for other in greeted:
+        pl.semaphore_signal(barrier, inc=1, device_id=other, device_id_type=MESH)
+    pl.semaphore_wait(barrier, len(greeted))
+
+    def kv_copy(d, source):
         return pltpu.make_async_remote_copy(
-            src_ref=kv_ref,
+            src_ref=source,
             dst_ref=kv_in.at[d - 1],
             send_sem=kv_send_sem.at[d - 1],
             recv_sem=kv_recv_sem.at[d - 1],
-            device_id=device(d),
+            device_id=device(SPAN) if d == SPAN else fellow(d),
             device_id_type=MESH,
         )
 
@@ -144,8 +149,24 @@
             device_id_type=MESH,
         )
 
-    for d in range(1, SPAN + 1):
-        kv_copy(d).start()
+    def advance(t):
+        for hop in range(SPAN - 1):
+            i = t - 1 - hop
+
+            @pl.when((i >= 0) & (i < steps))
+            def _():
+                hop_copy(hop, i).wait_recv()
+                for h in range(per):
+                    state = mm(map_ref[i, h], recv_ref[hop, i, h]) + off_ref[i, h]
+                    send_ref[hop + 1, i, h] = state.astype(BF16)
+                hop_copy(hop + 1, i).start()
+
+    kv_copy(SPAN, kv_ref).start()
+    for d in range(1, SPAN):
+
+        @pl.when(place + d < SPAN)
+        def _(d=d):
+            kv_copy(d, kv_ref).start()
 
     @pl.loop(0, steps)
     def _(i):
@@ -154,8 +175,19 @@
         )
         hop_copy(0, i).start()
 
-    for d in range(1, SPAN + 1):
-        kv_copy(d).wait_recv()
+        @pl.when(i == 1)
+        def _():
+            kv_copy(SPAN, kv_ref).wait_recv()
+            for d in range(1, SPAN):
+
+                @pl.when(place + d >= SPAN)
+                def _(d=d):
+                    kv_copy(d, kv_in.at[SPAN - 1]).start()
+
+        advance(i)
+
+    for d in range(1, SPAN):
+        kv_copy(d, kv_ref).wait_recv()
     group = aq_ref.shape[0] // kv_ref.shape[1]
 
     @pl.loop(0, kv_ref.shape[1])
@@ -170,17 +202,10 @@
             gate = agate_ref[g * group + j].astype(F32)
             att_ref[g * group + j] = (mixed / total / (1.0 + jnp.exp(-gate))).astype(BF16)
 
-    @pl.loop(0, (SPAN - 1) * steps)
-    def _(r):
-        hop, i = r // steps, r % steps
-        hop_copy(hop, i).wait_recv()
-        for h in range(per):
-            state = mm(map_ref[i, h], recv_ref[hop, i, h]) + off_ref[i, h]
-            send_ref[hop + 1, i, h] = state.astype(BF16)
-        hop_copy(hop + 1, i).start()
-
-    @pl.loop(0, steps)
-    def _(i):
+    @pl.loop(SPAN, steps + SPAN)
+    def _(t):
+        advance(t)
+        i = t - SPAN
         hop_copy(SPAN - 1, i).wait_recv()
         for h in range(per):
             core = base_ref[i, h] + mm(read_ref[i, h], recv_ref[SPAN - 1, i, h])
@@ -189,7 +214,7 @@
             out_ref[i * per + h] = (core * factor * (gate / (1.0 + jnp.exp(-gate)))).astype(BF16)
 
     for d in range(1, SPAN + 1):
-        kv_copy(d).wait_send()
+        kv_copy(d, kv_ref).wait_send()
 
     @pl.loop(0, SPAN * steps)
     def _(r):

time: 64.7 us -> 72.5 us (1.12)
  Pallas kernels: 50.8 us -> 58.6 us
    pallas_call x1, Pallas kernels: 50.8 us -> 58.6 us  [local(): pl.pallas_call(functools.partial(layer_kernel, per, ratio, attn_width **...]
where the time goes in v3:
time: 72.5 us; the launch traced here: 72.2 us
  Pallas kernels  58.6 us (81%)
  local copies, waits for them, and re-layouts  10.4 us (14%)
  other arithmetic  2.26 us (3%)
  between operations  0.88 us (1%)
    pallas_call x1, Pallas kernels, local(): pl.pallas_call(functools.partial(layer_kernel, per, ratio, attn_width **...  58.6 us
    unnamed x28, local copies, waits for them, and re-layouts  7.76 us

profile of v3, /device:TPU:0, one launch (start us, length us, event | category | flops | bytes accessed | tf_op | source)
XLA Modules:
  0.0 72.2 jit_solution(3680771581839475725)
XLA Ops:
  0.6 0.6 copy-done.10
  1.3 0.1 pad_dynamic-slice_fusion
  1.4 0.6 slice.21
  2.0 0.1 slice.19
  2.0 0.1 broadcast_in_dim.26
  2.1 0.1 slice.20
  2.2 0.6 slice.23
  2.8 1.3 %compare_convert_fusion = (f32[128]{0:T(128)S(1)}, f32[128]{0:T(128)S(1)}) fusion(s32[128]{0:T(128)S(1)} %slice.20, s32[]{:T(128)} %bitcast.8, s32[]{:T(128)} %bitcast.6), kind=kLoop, calls=%fused_computation.30 | loop fusion | flops 512 | bytes 1544 | tf_op jit(solution)/shard_map/convert_element_type | solution.py:262
  4.1 0.1 broadcast_in_dim.27
  4.2 0.6 copy-done.9
  4.9 0.1 copy.104
  5.0 0.2 reduce_window_sum.11
  5.3 0.5 copy-done.1
  5.8 0.2 multiply_reduce_fusion
  6.1 0.1 copy-done
  6.2 0.2 multiply_reduce_fusion.1
  6.5 0.7 copy-done.8
  7.2 0.1 constant_dynamic-update-slice_fusion
  7.4 0.1 fusion
  7.6 0.1 copy.111
  7.7 0.8 %copy-done.6 = bf16[128,2,256]{2,1,0:T(2,128)(2,1)S(1)} copy-done((bf16[128,2,256]{2,1,0:T(2,128)(2,1)S(1)}, bf16[128,2,256]{2,1,0:T(2,128)(2,1)}, u32[]{:S(2)}) %copy-start.6) | copy-done | bytes 131096
  8.6 0.1 broadcast_select_fusion.mask_ref
  8.7 0.1 copy_bitcast_fusion.4
  8.8 0.9 %copy-done.2 = bf16[128,16,128]{2,1,0:T(8,128)(2,1)S(1)} copy-done((bf16[128,16,128]{2,1,0:T(8,128)(2,1)S(1)}, bf16[128,16,128]{2,1,0:T(8,128)(2,1)}, u32[]{:S(2)}) %copy-start.2) | copy-done | bytes 524312
  9.7 0.2 copy-done.3
  9.9 0.3 copy_bitcast_fusion.2
  10.2 0.8 %copy-done.4 = bf16[128,8,256]{2,1,0:T(8,128)(2,1)S(1)} copy-done((bf16[128,8,256]{2,1,0:T(8,128)(2,1)S(1)}, bf16[128,8,256]{2,1,0:T(8,128)(2,1)}, u32[]{:S(2)}) %copy-start.4) | copy-done | bytes 524312
  10.9 0.2 copy-done.5
  11.1 0.2 copy_bitcast_fusion
  11.3 58.6 %layer.1 = (bf16[16,128,128]{2,1,0:T(8,128)(2,1)S(1)}, bf16[8,128,256]{2,1,0:T(8,128)(2,1)S(1)}) custom-call(bf16[8,128,128]{2,1,0:T(8,128)(2,1)S(1)} %get-tuple-element.27.q_ref, bf16[8,128,128]{2,1,0:T(8,128)(2,1)S(1)} %get-tuple-element.26.k_ref, bf16[16,128,128]{2,1,0:T(8,128)(2,1)S(1)} %get-tuple-element.25.v_ref, f32[4,128,24]{2,1,0:T(8,128)S(1)} %bitcast.46, ...), custom_call_target="tpu_custom_call" | custom-call | flops 8000000000 | bytes 8000000 | tf_op jit(solution)/shard_map/layer/pallas_call | solution.py:281
  70.0 1.1 %copy.118 = bf16[128,16,128]{2,1,0:T(8,128)(2,1)} copy(bf16[128,16,128]{2,0,1:T(8,128)(2,1)S(1)} %bitcast.45) | data formatting | bytes 1048576
  71.1 1.1 %copy.119 = bf16[128,8,256]{2,1,0:T(8,128)(2,1)} copy(bf16[128,8,256]{2,0,1:T(8,128)(2,1)S(1)} %bitcast.44) | data formatting | bytes 1048576
  (39 shorter events, 0.6 us)
Async XLA Ops:
  0.6 0.7 copy-start.10
  4.1 0.7 copy-start.9
  4.8 0.9 %copy-start.1 = (bf16[128,8,128]{2,1,0:T(8,128)(2,1)S(1)}, bf16[128,8,128]{2,1,0:T(8,128)(2,1)}, u32[]{:S(2)}) copy-start(bf16[128,8,128]{2,1,0:T(8,128)(2,1)} %param.11) | copy-start | bytes 786436
  5.2 1.0 %copy-start = (bf16[128,8,128]{2,1,0:T(8,128)(2,1)S(1)}, bf16[128,8,128]{2,1,0:T(8,128)(2,1)}, u32[]{:S(2)}) copy-start(bf16[128,8,128]{2,1,0:T(8,128)(2,1)} %param.12) | copy-start | bytes 786436
  6.5 0.7 copy-start.8
  7.5 0.9 %copy-start.6 = (bf16[128,2,256]{2,1,0:T(2,128)(2,1)S(1)}, bf16[128,2,256]{2,1,0:T(2,128)(2,1)}, u32[]{:S(2)}) copy-start(bf16[128,2,256]{2,1,0:T(2,128)(2,1)} %param.19) | copy-start | bytes 393220
  7.6 1.0 %copy-start.7 = (bf16[128,2,256]{2,1,0:T(2,128)(2,1)S(1)}, bf16[128,2,256]{2,1,0:T(2,128)(2,1)}, u32[]{:S(2)}) copy-start(bf16[128,2,256]{2,1,0:T(2,128)(2,1)} %param.18) | copy-start | bytes 393220
  8.7 1.0 %copy-start.2 = (bf16[128,16,128]{2,1,0:T(8,128)(2,1)S(1)}, bf16[128,16,128]{2,1,0:T(8,128)(2,1)}, u32[]{:S(2)}) copy-start(bf16[128,16,128]{2,1,0:T(8,128)(2,1)} %param.16) | copy-start | bytes 1572868
  8.7 1.2 %copy-start.3 = (bf16[128,16,128]{2,1,0:T(8,128)(2,1)S(1)}, bf16[128,16,128]{2,1,0:T(8,128)(2,1)}, u32[]{:S(2)}) copy-start(bf16[128,16,128]{2,1,0:T(8,128)(2,1)} %param.13) | copy-start | bytes 1572868
  9.9 1.0 %copy-start.4 = (bf16[128,8,256]{2,1,0:T(8,128)(2,1)S(1)}, bf16[128,8,256]{2,1,0:T(8,128)(2,1)}, u32[]{:S(2)}) copy-start(bf16[128,8,256]{2,1,0:T(8,128)(2,1)} %param.20) | copy-start | bytes 1572868
  9.9 1.2 %copy-start.5 = (bf16[128,8,256]{2,1,0:T(8,128)(2,1)S(1)}, bf16[128,8,256]{2,1,0:T(8,128)(2,1)}, u32[]{:S(2)}) copy-start(bf16[128,8,256]{2,1,0:T(8,128)(2,1)} %param.17) | copy-start | bytes 1572868

commit v4 on v2

--- a/solution.py
+++ b/solution.py
@@ -145,17 +145,37 @@
         )
 
     for d in range(1, SPAN + 1):
-        kv_copy(d).start()
+
+        @pl.when(me + d < size)
+        def _(d=d):
+            kv_copy(d).start()
+
+        @pl.when(me < d)
+        def _(d=d):
+            kv_in[d - 1] = jnp.zeros(kv_in.shape[1:], BF16)
+
+    @pl.when(me == 0)
+    def _():
+        @pl.loop(0, SPAN * steps)
+        def _(r):
+            recv_ref[r // steps, r % steps] = jnp.zeros(recv_ref.shape[2:], BF16)
 
     @pl.loop(0, steps)
     def _(i):
         chunk_step(
             i, per, ratio, q_ref, k_ref, v_ref, col_ref, row_ref, incl_ref, map_ref, off_ref, base_ref, read_ref, send_ref
         )
-        hop_copy(0, i).start()
+
+        @pl.when(me + 1 < size)
+        def _():
+            hop_copy(0, i).start()
 
     for d in range(1, SPAN + 1):
-        kv_copy(d).wait_recv()
+
+        @pl.when(me >= d)
+        def _(d=d):
+            kv_copy(d).wait_recv()
+
     group = aq_ref.shape[0] // kv_ref.shape[1]
 
     @pl.loop(0, kv_ref.shape[1])
@@ -173,15 +193,26 @@
     @pl.loop(0, (SPAN - 1) * steps)
     def _(r):
         hop, i = r // steps, r % steps
-        hop_copy(hop, i).wait_recv()
+
+        @pl.when(me > 0)
+        def _():
+            hop_copy(hop, i).wait_recv()
+
         for h in range(per):
             state = mm(map_ref[i, h], recv_ref[hop, i, h]) + off_ref[i, h]
             send_ref[hop + 1, i, h] = state.astype(BF16)
-        hop_copy(hop + 1, i).start()
+
+        @pl.when(me + 1 < size)
+        def _():
+            hop_copy(hop + 1, i).start()
 
     @pl.loop(0, steps)
     def _(i):
-        hop_copy(SPAN - 1, i).wait_recv()
+
+        @pl.when(me > 0)
+        def _():
+            hop_copy(SPAN - 1, i).wait_recv()
+
         for h in range(per):
             core = base_ref[i, h] + mm(read_ref[i, h], recv_ref[SPAN - 1, i, h])
             factor = lax.rsqrt(jnp.mean(core * core, axis=-1, keepdims=True) + 1e-06)
@@ -189,11 +220,16 @@
             out_ref[i * per + h] = (core * factor * (gate / (1.0 + jnp.exp(-gate)))).astype(BF16)
 
     for d in range(1, SPAN + 1):
-        kv_copy(d).wait_send()
-
-    @pl.loop(0, SPAN * steps)
-    def _(r):
-        hop_copy(r // steps, r % steps).wait_send()
+
+        @pl.when(me + d < size)
+        def _(d=d):
+            kv_copy(d).wait_send()
+
+    @pl.when(me + 1 < size)
+    def _():
+        @pl.loop(0, SPAN * steps)
+        def _(r):
+            hop_copy(r // steps, r % steps).wait_send()
 
 
 def local(

time: 64.7 us -> 62.4 us (0.964)
  the two profiles are of different devices: /device:TPU:0 before, /device:TPU:8 now
where the time goes in v4:
time: 62.4 us; the launch traced here: 62.1 us
  Pallas kernels  48.5 us (78%)
  local copies, waits for them, and re-layouts  10.4 us (17%)
  other arithmetic  2.26 us (4%)
  between operations  0.88 us (1%)
    pallas_call x1, Pallas kernels, local(): pl.pallas_call(functools.partial(layer_kernel, per, ratio, attn_width **...  48.5 us
    unnamed x28, local copies, waits for them, and re-layouts  7.76 us
    convert_element_type x1, other arithmetic, local(): lasting = (tok_doc == tok_doc[-1]).astype(F32)[:, None]  1.29 us

profile of v4, /device:TPU:8, one launch (start us, length us, event | category | flops | bytes accessed | tf_op | source)
XLA Modules:
  0.0 62.1 jit_solution(1435404721199563200)
XLA Ops:
  0.6 0.6 %copy-done.10 = s32[32]{0:T(128)S(1)} copy-done((s32[32]{0:T(128)S(1)}, s32[32]{0:T(128)}, u32[]{:S(2)}) %copy-start.10) | copy-done | bytes 152
  1.3 0.1 pad_dynamic-slice_fusion
  1.4 0.6 slice.21
  2.0 0.1 slice.19
  2.0 0.1 broadcast_in_dim.26
  2.1 0.1 slice.20
  2.2 0.6 slice.23
  2.8 1.3 %compare_convert_fusion = (f32[128]{0:T(128)S(1)}, f32[128]{0:T(128)S(1)}) fusion(s32[128]{0:T(128)S(1)} %slice.20, s32[]{:T(128)} %bitcast.8, s32[]{:T(128)} %bitcast.6), kind=kLoop, calls=%fused_computation.30 | loop fusion | flops 512 | bytes 1544 | tf_op jit(solution)/shard_map/convert_element_type | solution.py:273
  4.1 0.1 broadcast_in_dim.27
  4.2 0.6 %copy-done.9 = f32[128,16]{0,1:T(8,128)S(1)} copy-done((f32[128,16]{0,1:T(8,128)S(1)}, f32[128,16]{0,1:T(8,128)}, u32[]{:S(2)}) %copy-start.9) | copy-done | bytes 8216
  4.9 0.1 copy.104
  5.0 0.2 reduce_window_sum.11
  5.3 0.5 copy-done.1
  5.8 0.2 multiply_reduce_fusion
  6.1 0.1 copy-done
  6.2 0.2 multiply_reduce_fusion.1
  6.5 0.7 %copy-done.8 = f32[128,16]{0,1:T(8,128)S(1)} copy-done((f32[128,16]{0,1:T(8,128)S(1)}, f32[128,16]{0,1:T(8,128)}, u32[]{:S(2)}) %copy-start.8) | copy-done | bytes 8216
  7.2 0.1 constant_dynamic-update-slice_fusion
  7.4 0.1 fusion
  7.6 0.1 copy.111
  7.7 0.8 %copy-done.6 = bf16[128,2,256]{2,1,0:T(2,128)(2,1)S(1)} copy-done((bf16[128,2,256]{2,1,0:T(2,128)(2,1)S(1)}, bf16[128,2,256]{2,1,0:T(2,128)(2,1)}, u32[]{:S(2)}) %copy-start.6) | copy-done | bytes 131096
  8.6 0.1 broadcast_select_fusion.mask_ref
  8.7 0.1 copy_bitcast_fusion.4
  8.8 0.9 %copy-done.2 = bf16[128,16,128]{2,1,0:T(8,128)(2,1)S(1)} copy-done((bf16[128,16,128]{2,1,0:T(8,128)(2,1)S(1)}, bf16[128,16,128]{2,1,0:T(8,128)(2,1)}, u32[]{:S(2)}) %copy-start.2) | copy-done | bytes 524312
  9.7 0.2 copy-done.3
  9.9 0.3 copy_bitcast_fusion.2
  10.2 0.8 %copy-done.4 = bf16[128,8,256]{2,1,0:T(8,128)(2,1)S(1)} copy-done((bf16[128,8,256]{2,1,0:T(8,128)(2,1)S(1)}, bf16[128,8,256]{2,1,0:T(8,128)(2,1)}, u32[]{:S(2)}) %copy-start.4) | copy-done | bytes 524312
  10.9 0.2 copy-done.5
  11.1 0.2 copy_bitcast_fusion
  11.3 48.5 %layer.1 = (bf16[16,128,128]{2,1,0:T(8,128)(2,1)S(1)}, bf16[8,128,256]{2,1,0:T(8,128)(2,1)S(1)}) custom-call(bf16[8,128,128]{2,1,0:T(8,128)(2,1)S(1)} %get-tuple-element.27.q_ref, bf16[8,128,128]{2,1,0:T(8,128)(2,1)S(1)} %get-tuple-element.26.k_ref, bf16[16,128,128]{2,1,0:T(8,128)(2,1)S(1)} %get-tuple-element.25.v_ref, f32[4,128,24]{2,1,0:T(8,128)S(1)} %bitcast.46, ...), custom_call_target="tpu_custom_call" | custom-call | flops 8000000000 | bytes 8000000 | tf_op jit(solution)/shard_map/layer/pallas_call | solution.py:292
  59.9 1.1 %copy.118 = bf16[128,16,128]{2,1,0:T(8,128)(2,1)} copy(bf16[128,16,128]{2,0,1:T(8,128)(2,1)S(1)} %bitcast.45) | data formatting | bytes 1048576
  61.0 1.1 %copy.119 = bf16[128,8,256]{2,1,0:T(8,128)(2,1)} copy(bf16[128,8,256]{2,0,1:T(8,128)(2,1)S(1)} %bitcast.44) | data formatting | bytes 1048576
  (39 shorter events, 0.6 us)
Async XLA Ops:
  0.6 0.7 %copy-start.10 = (s32[32]{0:T(128)S(1)}, s32[32]{0:T(128)}, u32[]{:S(2)}) copy-start(s32[32]{0:T(128)} %param.21) | copy-start | bytes 388
  4.1 0.7 %copy-start.9 = (f32[128,16]{0,1:T(8,128)S(1)}, f32[128,16]{0,1:T(8,128)}, u32[]{:S(2)}) copy-start(f32[128,16]{0,1:T(8,128)} %param.14) | copy-start | bytes 24580
  4.8 0.9 %copy-start.1 = (bf16[128,8,128]{2,1,0:T(8,128)(2,1)S(1)}, bf16[128,8,128]{2,1,0:T(8,128)(2,1)}, u32[]{:S(2)}) copy-start(bf16[128,8,128]{2,1,0:T(8,128)(2,1)} %param.11) | copy-start | bytes 786436
  5.2 1.0 %copy-start = (bf16[128,8,128]{2,1,0:T(8,128)(2,1)S(1)}, bf16[128,8,128]{2,1,0:T(8,128)(2,1)}, u32[]{:S(2)}) copy-start(bf16[128,8,128]{2,1,0:T(8,128)(2,1)} %param.12) | copy-start | bytes 786436
  6.5 0.7 %copy-start.8 = (f32[128,16]{0,1:T(8,128)S(1)}, f32[128,16]{0,1:T(8,128)}, u32[]{:S(2)}) copy-start(f32[128,16]{0,1:T(8,128)} %param.15) | copy-start | bytes 24580
  7.5 0.9 %copy-start.6 = (bf16[128,2,256]{2,1,0:T(2,128)(2,1)S(1)}, bf16[128,2,256]{2,1,0:T(2,128)(2,1)}, u32[]{:S(2)}) copy-start(bf16[128,2,256]{2,1,0:T(2,128)(2,1)} %param.19) | copy-start | bytes 393220
  7.6 1.0 %copy-start.7 = (bf16[128,2,256]{2,1,0:T(2,128)(2,1)S(1)}, bf16[128,2,256]{2,1,0:T(2,128)(2,1)}, u32[]{:S(2)}) copy-start(bf16[128,2,256]{2,1,0:T(2,128)(2,1)} %param.18) | copy-start | bytes 393220
  8.7 1.0 %copy-start.2 = (bf16[128,16,128]{2,1,0:T(8,128)(2,1)S(1)}, bf16[128,16,128]{2,1,0:T(8,128)(2,1)}, u32[]{:S(2)}) copy-start(bf16[128,16,128]{2,1,0:T(8,128)(2,1)} %param.16) | copy-start | bytes 1572868
  8.7 1.2 %copy-start.3 = (bf16[128,16,128]{2,1,0:T(8,128)(2,1)S(1)}, bf16[128,16,128]{2,1,0:T(8,128)(2,1)}, u32[]{:S(2)}) copy-start(bf16[128,16,128]{2,1,0:T(8,128)(2,1)} %param.13) | copy-start | bytes 1572868
  9.9 1.0 %copy-start.4 = (bf16[128,8,256]{2,1,0:T(8,128)(2,1)S(1)}, bf16[128,8,256]{2,1,0:T(8,128)(2,1)}, u32[]{:S(2)}) copy-start(bf16[128,8,256]{2,1,0:T(8,128)(2,1)} %param.20) | copy-start | bytes 1572868
  9.9 1.2 %copy-start.5 = (bf16[128,8,256]{2,1,0:T(8,128)(2,1)S(1)}, bf16[128,8,256]{2,1,0:T(8,128)(2,1)}, u32[]{:S(2)}) copy-start(bf16[128,8,256]{2,1,0:T(8,128)(2,1)} %param.17) | copy-start | bytes 1572868

commit v5 on v4

--- a/solution.py
+++ b/solution.py
@@ -170,6 +170,22 @@
         def _():
             hop_copy(0, i).start()
 
+    @pl.loop(0, steps)
+    def _(r):
+        hop, i = r // steps, r % steps
+
+        @pl.when(me > 0)
+        def _():
+            hop_copy(hop, i).wait_recv()
+
+        for h in range(per):
+            state = mm(map_ref[i, h], recv_ref[hop, i, h]) + off_ref[i, h]
+            send_ref[hop + 1, i, h] = state.astype(BF16)
+
+        @pl.when(me + 1 < size)
+        def _():
+            hop_copy(hop + 1, i).start()
+
     for d in range(1, SPAN + 1):
 
         @pl.when(me >= d)
@@ -190,7 +206,7 @@
             gate = agate_ref[g * group + j].astype(F32)
             att_ref[g * group + j] = (mixed / total / (1.0 + jnp.exp(-gate))).astype(BF16)
 
-    @pl.loop(0, (SPAN - 1) * steps)
+    @pl.loop(steps, (SPAN - 1) * steps)
     def _(r):
         hop, i = r // steps, r % steps
 

time: 62.4 us -> 62.4 us (level)
  no operation moved by 1% of the time
where the time goes in v5:
time: 62.4 us; the launch traced here: 62.1 us
  Pallas kernels  48.5 us (78%)
  local copies, waits for them, and re-layouts  10.4 us (17%)
  other arithmetic  2.26 us (4%)
  between operations  0.88 us (1%)
    pallas_call x1, Pallas kernels, local(): pl.pallas_call(functools.partial(layer_kernel, per, ratio, attn_width **...  48.5 us
    unnamed x28, local copies, waits for them, and re-layouts  7.76 us
    convert_element_type x1, other arithmetic, local(): lasting = (tok_doc == tok_doc[-1]).astype(F32)[:, None]  1.29 us

profile of v5, /device:TPU:8, one launch (start us, length us, event | category | flops | bytes accessed | tf_op | source)
XLA Modules:
  0.0 62.1 jit_solution(15490380001494512460)
XLA Ops:
  0.6 0.6 %copy-done.10 = s32[32]{0:T(128)S(1)} copy-done((s32[32]{0:T(128)S(1)}, s32[32]{0:T(128)}, u32[]{:S(2)}) %copy-start.10) | copy-done | bytes 152
  1.3 0.1 pad_dynamic-slice_fusion
  1.4 0.6 slice.21
  2.0 0.1 slice.19
  2.0 0.1 broadcast_in_dim.26
  2.1 0.1 slice.20
  2.2 0.6 slice.23
  2.8 1.3 %compare_convert_fusion = (f32[128]{0:T(128)S(1)}, f32[128]{0:T(128)S(1)}) fusion(s32[128]{0:T(128)S(1)} %slice.20, s32[]{:T(128)} %bitcast.8, s32[]{:T(128)} %bitcast.6), kind=kLoop, calls=%fused_computation.30 | loop fusion | flops 512 | bytes 1544 | tf_op jit(solution)/shard_map/convert_element_type | solution.py:289
  4.1 0.1 broadcast_in_dim.27
  4.2 0.6 %copy-done.9 = f32[128,16]{0,1:T(8,128)S(1)} copy-done((f32[128,16]{0,1:T(8,128)S(1)}, f32[128,16]{0,1:T(8,128)}, u32[]{:S(2)}) %copy-start.9) | copy-done | bytes 8216
  4.9 0.1 copy.104
  5.0 0.2 reduce_window_sum.11
  5.3 0.5 copy-done.1
  5.8 0.2 multiply_reduce_fusion
  6.1 0.1 copy-done
  6.2 0.2 multiply_reduce_fusion.1
  6.5 0.7 %copy-done.8 = f32[128,16]{0,1:T(8,128)S(1)} copy-done((f32[128,16]{0,1:T(8,128)S(1)}, f32[128,16]{0,1:T(8,128)}, u32[]{:S(2)}) %copy-start.8) | copy-done | bytes 8216
  7.2 0.1 constant_dynamic-update-slice_fusion
  7.4 0.1 fusion
  7.6 0.1 copy.111
  7.7 0.8 %copy-done.6 = bf16[128,2,256]{2,1,0:T(2,128)(2,1)S(1)} copy-done((bf16[128,2,256]{2,1,0:T(2,128)(2,1)S(1)}, bf16[128,2,256]{2,1,0:T(2,128)(2,1)}, u32[]{:S(2)}) %copy-start.6) | copy-done | bytes 131096
  8.6 0.1 broadcast_select_fusion.mask_ref
  8.7 0.1 copy_bitcast_fusion.4
  8.8 0.9 %copy-done.2 = bf16[128,16,128]{2,1,0:T(8,128)(2,1)S(1)} copy-done((bf16[128,16,128]{2,1,0:T(8,128)(2,1)S(1)}, bf16[128,16,128]{2,1,0:T(8,128)(2,1)}, u32[]{:S(2)}) %copy-start.2) | copy-done | bytes 524312
  9.7 0.2 copy-done.3
  9.9 0.3 copy_bitcast_fusion.2
  10.2 0.8 %copy-done.4 = bf16[128,8,256]{2,1,0:T(8,128)(2,1)S(1)} copy-done((bf16[128,8,256]{2,1,0:T(8,128)(2,1)S(1)}, bf16[128,8,256]{2,1,0:T(8,128)(2,1)}, u32[]{:S(2)}) %copy-start.4) | copy-done | bytes 524312
  10.9 0.2 copy-done.5
  11.1 0.2 copy_bitcast_fusion
  11.3 48.5 %layer.1 = (bf16[16,128,128]{2,1,0:T(8,128)(2,1)S(1)}, bf16[8,128,256]{2,1,0:T(8,128)(2,1)S(1)}) custom-call(bf16[8,128,128]{2,1,0:T(8,128)(2,1)S(1)} %get-tuple-element.27.q_ref, bf16[8,128,128]{2,1,0:T(8,128)(2,1)S(1)} %get-tuple-element.26.k_ref, bf16[16,128,128]{2,1,0:T(8,128)(2,1)S(1)} %get-tuple-element.25.v_ref, f32[4,128,24]{2,1,0:T(8,128)S(1)} %bitcast.46, ...), custom_call_target="tpu_custom_call" | custom-call | flops 8000000000 | bytes 8000000 | tf_op jit(solution)/shard_map/layer/pallas_call | solution.py:308
  59.9 1.1 %copy.118 = bf16[128,16,128]{2,1,0:T(8,128)(2,1)} copy(bf16[128,16,128]{2,0,1:T(8,128)(2,1)S(1)} %bitcast.45) | data formatting | bytes 1048576
  61.0 1.1 %copy.119 = bf16[128,8,256]{2,1,0:T(8,128)(2,1)} copy(bf16[128,8,256]{2,0,1:T(8,128)(2,1)S(1)} %bitcast.44) | data formatting | bytes 1048576
  (39 shorter events, 0.6 us)
Async XLA Ops:
  0.6 0.7 %copy-start.10 = (s32[32]{0:T(128)S(1)}, s32[32]{0:T(128)}, u32[]{:S(2)}) copy-start(s32[32]{0:T(128)} %param.21) | copy-start | bytes 388
  4.1 0.7 %copy-start.9 = (f32[128,16]{0,1:T(8,128)S(1)}, f32[128,16]{0,1:T(8,128)}, u32[]{:S(2)}) copy-start(f32[128,16]{0,1:T(8,128)} %param.14) | copy-start | bytes 24580
  4.8 0.9 %copy-start.1 = (bf16[128,8,128]{2,1,0:T(8,128)(2,1)S(1)}, bf16[128,8,128]{2,1,0:T(8,128)(2,1)}, u32[]{:S(2)}) copy-start(bf16[128,8,128]{2,1,0:T(8,128)(2,1)} %param.11) | copy-start | bytes 786436
  5.2 1.0 %copy-start = (bf16[128,8,128]{2,1,0:T(8,128)(2,1)S(1)}, bf16[128,8,128]{2,1,0:T(8,128)(2,1)}, u32[]{:S(2)}) copy-start(bf16[128,8,128]{2,1,0:T(8,128)(2,1)} %param.12) | copy-start | bytes 786436
  6.5 0.7 %copy-start.8 = (f32[128,16]{0,1:T(8,128)S(1)}, f32[128,16]{0,1:T(8,128)}, u32[]{:S(2)}) copy-start(f32[128,16]{0,1:T(8,128)} %param.15) | copy-start | bytes 24580
  7.5 0.9 %copy-start.6 = (bf16[128,2,256]{2,1,0:T(2,128)(2,1)S(1)}, bf16[128,2,256]{2,1,0:T(2,128)(2,1)}, u32[]{:S(2)}) copy-start(bf16[128,2,256]{2,1,0:T(2,128)(2,1)} %param.19) | copy-start | bytes 393220
  7.6 1.0 %copy-start.7 = (bf16[128,2,256]{2,1,0:T(2,128)(2,1)S(1)}, bf16[128,2,256]{2,1,0:T(2,128)(2,1)}, u32[]{:S(2)}) copy-start(bf16[128,2,256]{2,1,0:T(2,128)(2,1)} %param.18) | copy-start | bytes 393220
  8.7 1.0 %copy-start.2 = (bf16[128,16,128]{2,1,0:T(8,128)(2,1)S(1)}, bf16[128,16,128]{2,1,0:T(8,128)(2,1)}, u32[]{:S(2)}) copy-start(bf16[128,16,128]{2,1,0:T(8,128)(2,1)} %param.16) | copy-start | bytes 1572868
  8.7 1.2 %copy-start.3 = (bf16[128,16,128]{2,1,0:T(8,128)(2,1)S(1)}, bf16[128,16,128]{2,1,0:T(8,128)(2,1)}, u32[]{:S(2)}) copy-start(bf16[128,16,128]{2,1,0:T(8,128)(2,1)} %param.13) | copy-start | bytes 1572868
  9.9 1.0 %copy-start.4 = (bf16[128,8,256]{2,1,0:T(8,128)(2,1)S(1)}, bf16[128,8,256]{2,1,0:T(8,128)(2,1)}, u32[]{:S(2)}) copy-start(bf16[128,8,256]{2,1,0:T(8,128)(2,1)} %param.20) | copy-start | bytes 1572868
  9.9 1.2 %copy-start.5 = (bf16[128,8,256]{2,1,0:T(8,128)(2,1)S(1)}, bf16[128,8,256]{2,1,0:T(8,128)(2,1)}, u32[]{:S(2)}) copy-start(bf16[128,8,256]{2,1,0:T(8,128)(2,1)} %param.17) | copy-start | bytes 1572868
